TPU v7x, 128 devices: a whole 4x4x4 slice. The times are simulated.
128 devices in a mesh: ctx: 16 (over y, x), rep: 8 (over z, core).
Axes of the slice: x: 4, y: 4, z: 4, core: 2. Of those that a mesh axis runs over, the one named last changes fastest.
Arguments:
- queries: bfloat16 [8, 2048, 4096], P('rep', 'ctx'), may hold values from -45 to 45
- cache_keys: bfloat16 [8, 2048, 1024], P('rep', 'ctx'), may hold values from -16 to 16
- cache_values: bfloat16 [8, 2048, 1024], P('rep', 'ctx'), may hold values from -6 to 6
- ssm_input: bfloat16 [8, 2048, 8192], P('rep', 'ctx'), may hold values from -6 to 6
- input_map: bfloat16 [8, 2048, 1024], P('rep', 'ctx'), may hold values from -0.03125 to 0.03125
- output_map: bfloat16 [8, 2048, 1024], P('rep', 'ctx'), may hold values from -6 to 6
- log_decay: float32 [8, 2048, 128], P('rep', 'ctx'), may hold values from -1.5 to 0
- skip_gain: float32 [128], replicated, may hold values from 0.25 to 1.75
- lengths: int32 [8], P('rep'), may hold values from 512 to 2048, as said below
- page_owner: int32 [8, 128, 1], P('rep', 'ctx'), may hold values from 0 to 7; in each aligned block of 8 rows (0 to 7, 8 to 15, ..., all dimensions but the last counted through in order) at most 4 rows name the same one
Outputs:
- attn_out: bfloat16 [8, 2048, 4096], P('rep', 'ctx')
- ssm_out: bfloat16 [8, 2048, 8192], P('rep', 'ctx')
- state_pool: bfloat16 [16, 8, 128, 64, 256], P('ctx', None, 'rep')
- page_pool: bfloat16 [16, 8, 8, 4, 2, 16, 1024], P('ctx', 'rep')
- page_ids: int32 [16, 8, 8, 4], P('ctx', 'rep')
Inputs may be any that keep to these rules, and one draw needn't show every extreme that they name: `lengths`: every length is a multiple of 128; some prompt has length 2048. `page_owner`: among the 8 pages of one device, at most 4 name the same owner; on some devices exactly 4 do.
All inputs are finite; a program needn't handle non-finite values.
Results may differ from a plain program's by a relative error of at most 0.013.
Values may be sent and summed in bfloat16 or wider, within the bound.
A program may use at most 384 MiB of HBM per device.

v0:
```python
import math

import jax
import jax.numpy as jnp
from jax import lax
from jax.sharding import PartitionSpec as P

HD = 128
GR = 4
PAGE = 16
CAP = 4


def prefix(x, axis, combine, identity):
    count, index = (lax.axis_size(axis), lax.axis_index(axis))
    everything = jax.tree.map(
        lambda part, kind: lax.all_gather(part.astype(kind), axis), x, (jnp.bfloat16, jnp.bfloat16)
    )
    start = jax.tree.map(
        lambda part, zero: jnp.broadcast_to(jnp.asarray(zero, part.dtype), part.shape), x, identity
    )

    def step(k, before):
        reached = k < index
        new = combine(
            before, jax.tree.map(lambda part, own: part[k].astype(own.dtype), everything, x)
        )
        return jax.tree.map(lambda a, b: jnp.where(reached, a, b), new, before)

    return lax.fori_loop(0, count, step, start)


def body(
    queries,
    cache_keys,
    cache_values,
    ssm_input,
    input_map,
    output_map,
    log_decay,
    skip_gain,
    lengths,
    page_owner,
):
    rep_count = lax.axis_size("rep")
    my_index = lax.axis_index("ctx")
    block_rows = queries.shape[1]
    half_rows = block_rows // 2
    length = lengths[0]
    query_rows = queries[0]
    key_rows = cache_keys[0]
    value_rows = cache_values[0]
    query_width = query_rows.shape[1]
    kv_width = key_rows.shape[1]
    kv_heads = kv_width // HD
    query_heads = query_width // HD
    groups = query_heads // kv_heads
    own_positions = my_index * block_rows + jnp.arange(block_rows, dtype=jnp.int32)
    scaling = 1.0 / math.sqrt(HD)
    query_four = query_rows.reshape(block_rows, kv_heads, groups, HD)
    query_parts = (query_four[:half_rows], query_four[half_rows:])
    position_parts = (own_positions[:half_rows], own_positions[half_rows:])

    def update(state, query_part, query_pos, key_block, value_block, key_pos):
        running_max, running_sum, weighted = state
        scores = (
            jnp.einsum("qkgd,tkd->kgqt", query_part, key_block, preferred_element_type=jnp.float32)
            * scaling
        )
        allowed = (key_pos[None, :] <= query_pos[:, None]) & (key_pos[None, :] < length)
        block_max = jnp.max(jnp.where(allowed, scores, -1e30), axis=-1)
        new_max = jnp.maximum(running_max, block_max)
        weights = jnp.where(allowed, jnp.exp(scores - new_max[..., None]), 0.0)
        rescale = jnp.exp(running_max - new_max)
        running_sum = running_sum * rescale + jnp.sum(weights, axis=-1)
        weighted = weighted * jnp.transpose(rescale, (2, 0, 1))[..., None] + jnp.einsum(
            "kgqt,tkd->qkgd",
            weights.astype(jnp.bfloat16),
            value_block,
            preferred_element_type=jnp.float32,
        )
        return (new_max, running_sum, weighted)

    def tile_pass(states, key_block, value_block, key_pos):
        updated = []
        for query_part in range(2):
            active = (jnp.min(key_pos) <= jnp.max(position_parts[query_part])) & (
                jnp.min(key_pos) < length
            )

            def compute(state):
                return update(
                    state,
                    query_parts[query_part],
                    position_parts[query_part],
                    key_block,
                    value_block,
                    key_pos,
                )

            def unchanged(state):
                return state

            updated.append(lax.cond(active, compute, unchanged, states[query_part]))
        return tuple(updated)

    empty_state = (
        jnp.full((kv_heads, groups, half_rows), -1e30, jnp.float32),
        jnp.zeros((kv_heads, groups, half_rows), jnp.float32),
        jnp.zeros((half_rows, kv_heads, groups, HD), jnp.float32),
    )
    states = (empty_state, empty_state)
    key_piece = lax.all_gather(key_rows, "ctx", axis=0, tiled=True)
    value_piece = lax.all_gather(value_rows, "ctx", axis=0, tiled=True)
    row_count = key_piece.shape[0]
    key_split = key_piece.reshape(row_count, kv_heads, HD)
    value_split = value_piece.reshape(row_count, kv_heads, HD)
    block_count = row_count // block_rows

    def advance(carried, block_data):
        key_block, value_block, first_row = block_data
        for key_part in range(2):
            lower_row = key_part * half_rows
            carried = tile_pass(
                carried,
                key_block[lower_row : lower_row + half_rows],
                value_block[lower_row : lower_row + half_rows],
                first_row + lower_row + jnp.arange(half_rows, dtype=jnp.int32),
            )
        return (carried, None)

    firsts = block_rows * jnp.arange(block_count, dtype=jnp.int32)
    states, _ = lax.scan(
        advance,
        states,
        (
            key_split.reshape(block_count, block_rows, kv_heads, HD),
            value_split.reshape(block_count, block_rows, kv_heads, HD),
            firsts,
        ),
    )
    finished = []
    for query_part in range(2):
        finished.append(
            states[query_part][2] / jnp.transpose(states[query_part][1], (2, 0, 1))[..., None]
        )
    attention_rows = (
        jnp.concatenate(finished, axis=0).reshape(block_rows, query_width).astype(jnp.bfloat16)
    )
    state_heads = log_decay.shape[2]
    head_width = ssm_input.shape[2] // state_heads
    state_width = input_map.shape[2] // GR
    head_group = state_heads // GR
    active_rows = (own_positions < length)[:, None]
    decays = jnp.where(active_rows, log_decay[0], 0.0)
    inputs = jnp.where(active_rows, ssm_input[0], jnp.zeros((), jnp.bfloat16))
    cumulative = jnp.cumsum(decays, axis=0)
    in_map = input_map[0].reshape(block_rows, GR, state_width)
    out_map = output_map[0].reshape(block_rows, GR, state_width)
    products = jnp.einsum("tgn,sgn->gts", out_map, in_map, preferred_element_type=jnp.float32)
    heads_cum = jnp.transpose(cumulative)
    spans_log = heads_cum[:, :, None] - heads_cum[:, None, :]
    order_index = jnp.arange(block_rows, dtype=jnp.int32)
    causal = order_index[None, :] <= order_index[:, None]
    fading = jnp.where(causal, jnp.exp(jnp.where(causal, spans_log, 0.0)), 0.0)
    fading = fading.reshape(GR, head_group, block_rows, block_rows)
    mixing = (products[:, None] * fading).astype(jnp.bfloat16)
    inputs_four = inputs.reshape(block_rows, GR, head_group, head_width)
    inner_part = jnp.einsum(
        "ghts,sghp->tghp", mixing, inputs_four, preferred_element_type=jnp.float32
    )
    to_end = jnp.exp(cumulative[-1][None, :] - cumulative).reshape(block_rows, GR, head_group)
    faded_input = (inputs_four.astype(jnp.float32) * to_end[..., None]).astype(jnp.bfloat16)
    block_state = jnp.einsum(
        "sghp,sgn->ghpn", faded_input, in_map, preferred_element_type=jnp.float32
    ).reshape(state_heads, head_width, state_width)

    def chain_link(earlier, later):
        return (earlier[0] + later[0], jnp.exp(later[0])[:, None, None] * earlier[1] + later[1])

    identity = (jnp.zeros_like(cumulative[-1]), jnp.zeros_like(block_state))
    entering = prefix((cumulative[-1], block_state), "ctx", chain_link, identity)[1]
    entering_low = entering.astype(jnp.bfloat16)
    carried_part = jnp.einsum(
        "tgn,ghpn->tghp",
        out_map,
        entering_low.reshape(GR, head_group, head_width, state_width),
        preferred_element_type=jnp.float32,
    )
    outer_part = jnp.exp(cumulative).reshape(block_rows, GR, head_group)[..., None] * carried_part
    skipped = skip_gain.reshape(GR, head_group)[None, :, :, None] * inputs_four.astype(jnp.float32)
    ssm_rows = (
        (inner_part + outer_part + skipped)
        .reshape(block_rows, state_heads * head_width)
        .astype(jnp.bfloat16)
    )
    leaving = (jnp.exp(cumulative[-1])[:, None, None] * entering + block_state).astype(jnp.bfloat16)
    page_rows = block_rows // PAGE
    stacked = jnp.stack(
        [
            key_rows.reshape(page_rows, PAGE, kv_width),
            value_rows.reshape(page_rows, PAGE, kv_width),
        ],
        axis=1,
    )
    page_number = my_index * page_rows + jnp.arange(page_rows, dtype=jnp.int32)
    alive_page = page_number * PAGE < length
    stacked = jnp.where(alive_page[:, None, None, None], stacked, jnp.zeros((), jnp.bfloat16))
    owners = page_owner[0, :, 0]
    owner_onehot_mask = (owners[:, None] == jnp.arange(rep_count, dtype=jnp.int32)[None, :]).astype(
        jnp.int32
    )
    ranking = jnp.cumsum(owner_onehot_mask, axis=0) - owner_onehot_mask
    slot_index = jnp.sum(ranking * owner_onehot_mask, axis=1)
    selector = jnp.transpose(owner_onehot_mask)[:, None, :] * (
        slot_index[None, None, :] == jnp.arange(CAP, dtype=jnp.int32)[None, :, None]
    ).astype(jnp.int32)
    buffer = jnp.einsum(
        "oqp,px->oqx",
        selector.astype(jnp.bfloat16),
        stacked.reshape(page_rows, 2 * PAGE * kv_width),
        preferred_element_type=jnp.float32,
    ).astype(jnp.bfloat16)
    buffer = buffer.reshape(rep_count, CAP, 2, PAGE, kv_width)
    labels = jnp.where(alive_page, page_number, -1) + 1
    page_ids = jnp.sum(selector * labels[None, None, :], axis=2) - 1
    state_share = leaving.reshape(rep_count, state_heads // rep_count, head_width, state_width)
    got_pages, got_ids, got_states = (
        lax.all_to_all(buffer, "rep", split_axis=0, concat_axis=0, tiled=True),
        lax.all_to_all(page_ids, "rep", split_axis=0, concat_axis=0, tiled=True),
        lax.all_to_all(state_share, "rep", split_axis=0, concat_axis=0, tiled=True),
    )
    return (
        attention_rows[None],
        ssm_rows[None],
        got_states[None],
        got_pages[None, None],
        got_ids[None, None],
    )


def solution(mesh):
    placed = (
        P("rep", "ctx", None),
        P("rep", "ctx", None),
        P("rep", "ctx", None),
        P("rep", "ctx", None),
        P("rep", "ctx", None),
        P("rep", "ctx", None),
        P("rep", "ctx", None),
        P(),
        P("rep"),
        P("rep", "ctx", None),
    )
    return jax.shard_map(
        body,
        mesh=mesh,
        in_specs=placed,
        out_specs=(
            P("rep", "ctx", None),
            P("rep", "ctx", None),
            P("ctx", None, "rep", None, None),
            P("ctx", "rep", None, None, None, None, None),
            P("ctx", "rep", None, None),
        ),
        check_vma=False,
    )
```

profile of v0, /device:TPU:62, one launch (start us, length us, event | category | flops | bytes accessed | tf_op | source)
XLA Modules:
  0.0 1311.4 jit_solution(8381116581951807910)
XLA Ops:
  42.9 17.8 %all-gather.2 = bf16[16,1,128]{2,1,0:T(2,128)(2,1)S(1)} all-gather(bf16[1,1,128]{2,1,0:T(2,128)(2,1)S(1)} %convert_bitcast_fusion), channel_id=1, replica_groups=mesh['ctx'=16,'rep'=8] {'ctx'}, dimensions={0}, use_global_device_ids=true | all-gather | bytes 4352 | tf_op jit(solution)/shard_map/all_gather | solution.py:17
  80.1 34.6 %all-gather.11.cloned.1.call-done = bf16[1,2048,1024]{2,1,0:T(8,128)(2,1)} async-done(((bf16[1,128,1024]{2,1,0:T(8,128)(2,1)}), bf16[1,2048,1024]{2,1,0:T(8,128)(2,1)}) %all-gather.11.cloned.1.call-update) | async-done | bytes 4194320 | tf_op jit(solution)/shard_map/all_gather | solution.py:114
  119.9 365.2 %all-gather.7.cloned.1.call-done = bf16[16,128,64,256]{3,2,1,0:T(8,128)(2,1)} async-done(((bf16[1,128,64,256]{3,2,1,0:T(8,128)(2,1)}), bf16[16,128,64,256]{3,2,1,0:T(8,128)(2,1)}) %all-gather.7.cloned.1.call-update) | async-done | bytes 67108880 | tf_op jit(solution)/shard_map/all_gather | solution.py:17
  485.1 123.6 %while.36 = (s32[]{:T(128)}, f32[128,64,256]{2,1,0:T(8,128)}, s32[]{:T(128)}, bf16[16,128]{1,0:T(8,128)(2,1)S(1)}, bf16[16,128,64,256]{3,2,1,0:T(8,128)(2,1)}, /*index=5*/s32[]{:T(128)}, s32[]{:T(128)}) while((s32[]{:T(128)}, f32[128,64,256]{2,1,0:T(8,128)}, s32[]{:T(128)}, bf16[16,128]{1,0:T(8,128)(2,1)S(1)}, ...), condition=%wide.region_24.25_spmd.clone, body=%wide.region_23.24_spmd.clone.sunk | while | flops 10485892 | bytes 20972904 | solution.py:30
  491.1 7.8 fusion.97
  499.0 7.8 fusion.97
  506.8 7.8 fusion.97
  514.7 7.8 fusion.97
  522.5 7.8 fusion.97
  530.3 7.8 fusion.97
  538.2 7.8 fusion.97
  546.0 7.8 fusion.97
  553.8 7.8 fusion.97
  561.7 7.8 fusion.97
  569.5 7.8 fusion.97
  577.4 7.8 fusion.97
  585.2 7.8 fusion.97
  593.0 7.8 fusion.97
  600.9 7.8 fusion.97
  608.7 12.1 fusion.51
  627.8 654.7 %while.35 = (s32[]{:T(128)}, f32[8,4,64]{2,1,0:T(4,128)S(1)}, f32[8,4,64]{2,1,0:T(4,128)}, f32[64,8,4,128]{3,0,2,1:T(8,128)S(1)}, f32[8,4,64]{2,1,0:T(4,128)}, /...) while((s32[]{:T(128)}, f32[8,4,64]{2,1,0:T(4,128)S(1)}, ...), condition=%wide.region_21.22_spmd, body=%wide.region_2.21_spmd.sunk | while | flops 275309184 | bytes 20517688 | solution.py:133
  637.4 7.3 conditional.10
  678.7 7.3 conditional.10
  719.9 7.3 conditional.10
  761.2 7.3 conditional.10
  802.4 7.3 conditional.10
  843.6 7.3 conditional.10
  884.9 7.3 conditional.10
  926.1 7.3 conditional.10
  1049.8 7.3 conditional.10
  1091.0 7.3 conditional.10
  1173.5 7.3 conditional.10
  (814 shorter events, 919.3 us)
Async XLA Ops:
  7.2 6.8 copy-start.7
  7.2 66.7 %all-gather.9.cloned.1.call-start = ((), (), s32[]{:S(2)}) async-start(), calls=%async_computation.4 | async-start | bytes 4456448 | tf_op jit(solution)/shard_map/all_gather | solution.py:113
  7.9 106.8 %all-gather.11.cloned.1.call-start = ((), (), s32[]{:S(2)}) async-start(), calls=%async_computation.5 | async-start | bytes 4456448 | tf_op jit(solution)/shard_map/all_gather | solution.py:114
  8.7 476.4 %all-gather.7.cloned.1.call-start = ((), (), s32[]{:S(2)}) async-start(), calls=%async_computation.3 | async-start | bytes 71303168 | tf_op jit(solution)/shard_map/all_gather | solution.py:17
  9.4 57.6 %copy-start.10 = (pred[128]{0:T(512)(128)(4,1)}, pred[128]{0:T(512)(128)(4,1)S(1)}, u32[]{:S(2)}) copy-start(pred[128]{0:T(512)(128)(4,1)S(1)} %broadcast_compare_fusion.4) | copy-start | bytes 388
  13.9 6.8 copy-start.2
  20.7 0.7 copy-start.9
  20.7 7.3 copy-start.5
  20.7 7.3 copy-start.6
  22.5 9.2 all-to-all-start.2
  31.7 42.1 %all-to-all-start.1 = ((bf16[8,4,2,16,1024]{4,3,2,1,0:T(8,128)(2,1)}), bf16[8,4,2,16,1024]{4,3,2,1,0:T(8,128)(2,1)S(1)}, u32[]{:S(2)}, u32[]{:S(2)}) async-start(bf16[8,4,2,16,1024]{4,3,2,1,0:T(8,128)(2,1)} %copy.85), calls=%async_computation.1 | async-start | bytes 4194304 | tf_op jit(solution)/shard_map/all_to_all | solution.py:229
  73.9 6.2 copy-start
  620.8 677.9 %all-to-all-start = ((bf16[8,16,64,256]{3,2,1,0:T(8,128)(2,1)}), bf16[8,16,64,256]{3,2,1,0:T(8,128)(2,1)}, u32[]{:S(2)}, u32[]{:S(2)}) async-start(bf16[8,16,64,256]{3,2,1,0:T(8,128)(2,1)} %bitcast.202), calls=%async_computation | async-start | bytes 8388608 | tf_op jit(solution)/shard_map/all_to_all | solution.py:231
  1282.5 6.0 copy-start.4
  1282.5 6.0 copy-start.8
  1282.5 6.0 copy-start.11
  1282.5 6.0 copy-start.12
  1284.0 4.5 copy-start.3
  1298.7 4.9 copy-start.1
Sparse Core Ops, SparseCore 0:
  10.2 51.3 all-gather.8
  63.6 50.9 all-gather.10
  116.8 368.2 all-gather.6
where the time goes:
time: 1330 us; the launch traced here: 1310 us
  other arithmetic  449 us (34%)
  waiting for transfers between devices  401 us (30%)
  local copies, waits for them, and re-layouts  141 us (11%)
  loops' own time  140 us (11%)
  matrix products  132 us (10%)
  blocking collectives  17.8 us (1%)
  starting transfers between devices  15.5 us (1%)
  between operations  14.7 us (1%)
    all_gather x1, waiting for transfers between devices, prefix(): lax.all_gather(part.astype(kind), axis)  365 us
    another operation x1, loops' own time, body(): lax.scan(advance, states, (key_split.reshape(block_count, block_rows, kv_...  137 us
    select_n x16, other arithmetic, step(): return jax.tree.map(lambda a, b: jnp.where(reached, a, b), new, before)  123 us
    add x63, other arithmetic, update(): running_sum = running_sum * rescale + jnp.sum(weights, axis=-1)  84.5 us
    lt x63, other arithmetic, update(): key_pos[None, :] < length  82.9 us
    dot_general x63, matrix products, update(): jnp.einsum('qkgd,tkd->kgqt', query_part, key_block, preferred_element_typ...  69.5 us
    and x63, other arithmetic, update(): (key_pos[None, :] <= query_pos[:, None]) & (key_pos[None, :] < length)  47.3 us
    dot_general x63, matrix products, update(): jnp.einsum('kgqt,tkd->qkgd', weights.astype(jnp.bfloat16), value_block, p...  42.8 us
  transfers between devices with their start and end apart: 6, of which 3 were waited for; matrix products, arithmetic and copies ran while one was open for 44% of the time, Pallas kernels for 0%

commit v1 on v0

v1 whole, which is shorter than its diff:
```python
import functools
import math

import jax
import jax.numpy as jnp
from jax import lax
from jax.experimental import pallas as pl
from jax.experimental.pallas import tpu as pltpu
from jax.sharding import PartitionSpec as P

HD = 128
GR = 4
PAGE = 16
CAP = 4
MP = 64
NS = 256
ROWS = 128
HG = 32
GW = HG * MP
PIECE = 8 * MP
MESH = pl.DeviceIdType.MESH
F32 = jnp.float32
BF16 = jnp.bfloat16


def mod4(v):
    return lax.rem(v + 8, 4)


def ssm_kernel(
    x_ref, b_ref, c_ref, ef_ref, cumt_ref, cumg_ref, ecum_ref, wg_ref, live_ref, skip_ref,
    out_ref, pool_ref,
    ft, ft_in, b_in, w_in, part, wprod, t_out, t_in, w4_in, e0_out, e0_in, e_out, e_in,
    inner, snap,
    s_ft, r_ft, s_b, r_b, s_w, r_w, s_t, r_t, s_w4, r_w4, s_e0, r_e0, s_e, r_e, s_p, r_p, l_p,
):
    ctx = lax.axis_index("ctx")
    rep = lax.axis_index("rep")
    mx = lax.rem(ctx, 4)
    my = ctx // 4
    mz = rep // 2

    def row_peer(j):
        return (my * 4 + j, rep)

    def col_peer(j):
        return (j * 4 + mx, rep)

    barrier = pltpu.get_barrier_semaphore()
    for i in range(1, 4):
        pl.semaphore_signal(barrier, inc=1, device_id=row_peer(mod4(mx + i)), device_id_type=MESH)
        pl.semaphore_signal(barrier, inc=1, device_id=col_peer(mod4(my + i)), device_id_type=MESH)
    for i in range(1, 8):
        pl.semaphore_signal(
            barrier, inc=1, device_id=(ctx, lax.rem(rep + i, 8)), device_id_type=MESH
        )
    pl.semaphore_wait(barrier, 13)

    def remote(src, dst, send, recv, device):
        return pltpu.make_async_remote_copy(
            src_ref=src, dst_ref=dst, send_sem=send, recv_sem=recv, device_id=device,
            device_id_type=MESH,
        )

    def rows_of(piece):
        return pl.ds(pl.multiple_of(piece * PIECE, PIECE), PIECE)

    def fade(j):
        def pair(p, carry):
            lanes = pl.ds(pl.multiple_of(j * GW + p * 128, 128), 128)
            turned = jnp.transpose(x_ref[:, lanes].astype(F32))
            factor = jnp.broadcast_to(
                ef_ref[j, pl.ds(2 * p, 2), :][:, None, :], (2, MP, ROWS)
            ).reshape(128, ROWS)
            ft[j, pl.ds(pl.multiple_of(p * 128, 128), 128), :] = (turned * factor).astype(BF16)
            return carry

        lax.fori_loop(0, HG // 2, pair, 0, unroll=4)

    sent = []
    for i in (1, 3, 2):
        j = mod4(mx + i)
        fade(j)
        lanes = pl.ds(pl.multiple_of(j * NS, NS), NS)
        for c in (
            remote(ft.at[j], ft_in.at[mx], s_ft.at[i], r_ft.at[mx], row_peer(j)),
            remote(b_ref.at[:, lanes], b_in.at[mx], s_b.at[i], r_b.at[mx], row_peer(j)),
            remote(wg_ref.at[j], w_in.at[mx], s_w.at[i], r_w.at[mx], row_peer(j)),
        ):
            c.start()
            sent.append(c)
    fade(mx)
    ft_in[mx] = ft[mx]
    b_in[mx] = b_ref[:, pl.ds(pl.multiple_of(mx * NS, NS), NS)]
    w_in[mx] = wg_ref[mx]

    live = live_ref[0:1, :]
    lane = lax.broadcasted_iota(jnp.int32, (ROWS, 128), 1)
    line = lax.broadcasted_iota(jnp.int32, (ROWS, 128), 0)
    causal = lane <= line
    low = lane < MP

    def inner_group(g, carry):
        lanes = pl.ds(pl.multiple_of(g * NS, NS), NS)
        products = lax.dot_general(
            c_ref[:, lanes], b_ref[:, lanes], (((1,), (1,)), ((), ())),
            preferred_element_type=F32,
        )
        products = jnp.where(causal, products * live, 0.0)
        for p in range(HG // 2):
            at = pl.ds(pl.multiple_of(g * GW + p * 128, 128), 128)
            values = x_ref[:, at]
            halves = []
            for k in range(2):
                h = 2 * p + k
                column = cumg_ref[g, :, h : h + 1]
                row = cumt_ref[g, h : h + 1, :]
                mix = (products * jnp.exp(jnp.minimum(column - row, 0.0))).astype(BF16)
                halves.append(jnp.dot(mix, values, preferred_element_type=F32))
            inner[:, at] = jnp.where(low, halves[0], halves[1]) + skip_ref[0:1, at] * (
                values.astype(F32) * live
            )
        return carry

    lax.fori_loop(0, GR, inner_group, 0)

    for i in (1, 3, 2):
        j = mod4(mx + i)
        remote(ft.at[j], ft_in.at[j], s_ft.at[i], r_ft.at[j], row_peer(j)).wait_recv()
        remote(b_in.at[j], b_in.at[j], s_b.at[i], r_b.at[j], row_peer(j)).wait_recv()
        remote(wg_ref.at[j], w_in.at[j], s_w.at[i], r_w.at[j], row_peer(j)).wait_recv()

    running = w_in[0]
    for k in range(1, 4):
        wprod[k - 1] = running
        running = running * w_in[k]
    wprod[3] = running

    def widen(rows, heads):
        both = jnp.concatenate([rows, rows], axis=1)
        return jnp.broadcast_to(both[:, None, :], (heads, MP, NS)).reshape(heads * MP, NS)

    def scan_piece(piece):
        def chunk(c, carry):
            first = piece * 8 + c * 4
            at = pl.ds(pl.multiple_of(first * MP, 256), 256)
            state = jnp.dot(ft_in[0, at, :], b_in[0], preferred_element_type=F32)
            for k in range(1, 4):
                part[k - 1, at, :] = state
                state = state * widen(w_in[k, pl.ds(first, 4), :], 4) + jnp.dot(
                    ft_in[k, at, :], b_in[k], preferred_element_type=F32
                )
            t_out[at, :] = state.astype(BF16)
            return carry

        lax.fori_loop(0, 2, chunk, 0)

    for i in (1, 3, 2):
        j = mod4(my + i)
        scan_piece(j)
        heads = pl.ds(pl.multiple_of(j * 8, 8), 8)
        for c in (
            remote(t_out.at[rows_of(j), :], t_in.at[my], s_t.at[i], r_t.at[my], col_peer(j)),
            remote(wprod.at[3, heads, :], w4_in.at[my], s_w4.at[i], r_w4.at[my], col_peer(j)),
        ):
            c.start()
            sent.append(c)
    scan_piece(my)
    t_in[my] = t_out[rows_of(my), :]
    w4_in[my] = wprod[3, pl.ds(pl.multiple_of(my * 8, 8), 8), :]
    for i in (1, 3, 2):
        j = mod4(my + i)
        remote(t_in.at[j], t_in.at[j], s_t.at[i], r_t.at[j], col_peer(j)).wait_recv()
        remote(w4_in.at[j], w4_in.at[j], s_w4.at[i], r_w4.at[j], col_peer(j)).wait_recv()

    def starts(c, carry):
        first = c * 4
        at = pl.ds(pl.multiple_of(first * MP, 256), 256)
        state = jnp.zeros((256, NS), F32)
        for k in range(4):
            e0_out[k, at, :] = state.astype(BF16)
            if k < 3:
                state = state * widen(w4_in[k, pl.ds(first, 4), :], 4) + t_in[k, at, :].astype(F32)
        return carry

    lax.fori_loop(0, 2, starts, 0)
    for i in (1, 3, 2):
        j = mod4(my + i)
        c = remote(e0_out.at[j], e0_in.at[my], s_e0.at[i], r_e0.at[my], col_peer(j))
        c.start()
        sent.append(c)
    e0_in[my] = e0_out[my]

    for t, d in enumerate((0, 1, 3, 2)):
        piece = mod4(my + d)
        if d != 0:
            remote(
                e0_in.at[piece], e0_in.at[piece], s_e0.at[d], r_e0.at[piece], col_peer(piece)
            ).wait_recv()

        def enter(c, carry):
            first = piece * 8 + c * 4
            at = pl.ds(pl.multiple_of(first * MP, 256), 256)
            low_start = e0_in[piece, pl.ds(pl.multiple_of(c * 256, 256), 256), :]
            start = low_start.astype(F32)
            e_out[0, at, :] = low_start
            for k in range(1, 4):
                e_out[k, at, :] = (
                    start * widen(wprod[k - 1, pl.ds(first, 4), :], 4) + part[k - 1, at, :]
                ).astype(BF16)
            return carry

        lax.fori_loop(0, 2, enter, 0)
        at = rows_of(piece)
        for i in (1, 3, 2):
            j = mod4(mx + i)
            c = remote(
                e_out.at[j, at, :], e_in.at[mx, at, :], s_e.at[i, d], r_e.at[mx, d], row_peer(j)
            )
            c.start()
            sent.append(c)
        e_in[mx, at, :] = e_out[mx, at, :]

    for d in (0, 1, 3, 2):
        piece = mod4(my + d)
        at = rows_of(piece)
        for s in range(4):
            j = mod4(mx + mz + s)

            @pl.when(j != mx)
            def _():
                remote(
                    e_in.at[j, at, :], e_in.at[j, at, :], s_e.at[1, d], r_e.at[j, d], row_peer(j)
                ).wait_recv()

            lanes = pl.ds(pl.multiple_of(j * NS, NS), NS)

            def finish(c, carry):
                sub = pl.ds(pl.multiple_of(piece * PIECE + c * 256, 256), 256)
                entering = e_in[j, sub, :]
                carried = lax.dot_general(
                    c_ref[:, lanes], entering, (((1,), (1,)), ((), ())),
                    preferred_element_type=F32,
                )
                for q in range(2):
                    scale = [
                        jnp.broadcast_to(
                            ecum_ref[j, piece * 2 + c, :, 2 * q + k : 2 * q + k + 1], (ROWS, 128)
                        )
                        for k in range(2)
                    ]
                    wide = pl.ds(
                        pl.multiple_of(j * GW + piece * PIECE + c * 256 + q * 128, 128), 128
                    )
                    out_ref[:, wide] = (
                        inner[:, wide]
                        + jnp.where(low, scale[0], scale[1]) * carried[:, q * 128 : q * 128 + 128]
                    ).astype(BF16)
                own = jnp.dot(ft[j, sub, :], b_ref[:, lanes], preferred_element_type=F32)
                factor = widen(wg_ref[j, pl.ds(piece * 8 + c * 4, 4), :], 4)
                leaving = (own + factor * entering.astype(F32)).astype(BF16)
                snap[j, pl.ds(piece * 8 + c * 4, 4)] = leaving.reshape(4, MP, NS)
                return carry

            lax.fori_loop(0, 2, finish, 0)
            owner = 2 * j + piece // 2
            half = lax.rem(piece, 2)
            source = snap.at[j, pl.ds(pl.multiple_of(piece * 8, 8), 8)]
            target = pool_ref.at[rep, pl.ds(pl.multiple_of(half * 8, 8), 8)]

            @pl.when(owner != rep)
            def _():
                remote(
                    source, target, s_p.at[s, d], r_p.at[rep, half], (ctx, owner)
                ).start()

            @pl.when(owner == rep)
            def _():
                pltpu.make_async_copy(source, target, l_p.at[half]).start()

    for c in sent:
        c.wait_send()
    for d in range(4):
        piece = mod4(my + d)
        for s in range(4):
            j = mod4(mx + mz + s)
            owner = 2 * j + piece // 2
            half = lax.rem(piece, 2)
            source = snap.at[j, pl.ds(pl.multiple_of(piece * 8, 8), 8)]
            target = pool_ref.at[rep, pl.ds(pl.multiple_of(half * 8, 8), 8)]

            @pl.when(owner != rep)
            def _():
                remote(
                    source, target, s_p.at[s, d], r_p.at[rep, half], (ctx, owner)
                ).wait_send()

            @pl.when(owner == rep)
            def _():
                pltpu.make_async_copy(source, target, l_p.at[half]).wait()
    for i in range(1, 8):
        other = lax.rem(rep + i, 8)
        for half in range(2):
            target = pool_ref.at[other, pl.ds(half * 8, 8)]
            remote(target, target, s_p.at[0, 0], r_p.at[other, half], (ctx, other)).wait_recv()


def ssm_call(x, b, c, ef, cumt, cumg, ecum, wg, live, skip):
    dma = pltpu.SemaphoreType.DMA
    vmem = pl.BlockSpec(memory_space=pltpu.VMEM)
    return pl.pallas_call(
        ssm_kernel,
        out_shape=(
            jax.ShapeDtypeStruct((ROWS, GR * GW), BF16),
            jax.ShapeDtypeStruct((8, 16, MP, NS), BF16),
        ),
        in_specs=[vmem] * 10,
        out_specs=(vmem, pl.BlockSpec(memory_space=pl.ANY)),
        scratch_shapes=[
            pltpu.VMEM((4, GW, ROWS), BF16),
            pltpu.VMEM((4, GW, ROWS), BF16),
            pltpu.VMEM((4, ROWS, NS), BF16),
            pltpu.VMEM((4, HG, 128), F32),
            pltpu.VMEM((3, GW, NS), F32),
            pltpu.VMEM((4, HG, 128), F32),
            pltpu.VMEM((GW, NS), BF16),
            pltpu.VMEM((4, PIECE, NS), BF16),
            pltpu.VMEM((4, 8, 128), F32),
            pltpu.VMEM((4, PIECE, NS), BF16),
            pltpu.VMEM((4, PIECE, NS), BF16),
            pltpu.VMEM((4, GW, NS), BF16),
            pltpu.VMEM((4, GW, NS), BF16),
            pltpu.VMEM((ROWS, GR * GW), F32),
            pltpu.VMEM((4, HG, MP, NS), BF16),
            dma((4,)), dma((4,)), dma((4,)), dma((4,)), dma((4,)), dma((4,)),
            dma((4,)), dma((4,)), dma((4,)), dma((4,)), dma((4,)), dma((4,)),
            dma((4, 4)), dma((4, 4)), dma((4, 4)), dma((8, 2)), dma((2,)),
        ],
        compiler_params=pltpu.CompilerParams(
            collective_id=0, has_side_effects=True, vmem_limit_bytes=56 << 20
        ),
        name="ssm_exchange",
    )(x, b, c, ef, cumt, cumg, ecum, wg, live, skip)


def attend_kernel(limits, q_ref, kv_ref, out_ref):
    first = limits[0]
    length = limits[1]
    tile = 256
    tiles = (jnp.minimum(first + ROWS, length) + tile - 1) // tile
    scale = math.log2(math.e) / math.sqrt(HD)
    query_pos = first + lax.broadcasted_iota(jnp.int32, (ROWS, tile), 0)
    key_off = lax.broadcasted_iota(jnp.int32, (ROWS, tile), 1)
    for k in range(8):
        query = jnp.concatenate(
            [q_ref[:, (4 * k + i) * HD : (4 * k + i + 1) * HD] for i in range(4)], axis=0
        )

        def step(t, carry):
            top, total, acc = carry
            at = pl.ds(pl.multiple_of(t * tile, tile), tile)
            scores = lax.dot_general(
                query, kv_ref[at, k * HD : (k + 1) * HD], (((1,), (1,)), ((), ())),
                preferred_element_type=F32,
            )
            key_pos = key_off + t * tile
            bias = jnp.where((key_pos <= query_pos) & (key_pos < length), 0.0, -1e30)
            scores = scores + jnp.concatenate([bias] * 4, axis=0)
            new_top = jnp.maximum(top, jnp.max(scores, axis=1, keepdims=True))
            weights = jnp.exp2((scores - new_top) * scale)
            fix = jnp.exp2((top - new_top) * scale)
            total = total * fix + jnp.sum(weights, axis=1, keepdims=True)
            acc = acc * fix + jnp.dot(
                weights.astype(BF16), kv_ref[at, 1024 + k * HD : 1024 + (k + 1) * HD],
                preferred_element_type=F32,
            )
            return new_top, total, acc

        top, total, acc = lax.fori_loop(
            0, tiles, step,
            (
                jnp.full((4 * ROWS, 1), -1e30, F32),
                jnp.zeros((4 * ROWS, 1), F32),
                jnp.zeros((4 * ROWS, HD), F32),
            ),
        )
        result = (acc / total).astype(BF16)
        for i in range(4):
            out_ref[:, (4 * k + i) * HD : (4 * k + i + 1) * HD] = result[i * ROWS : (i + 1) * ROWS]


def attend_call(limits, q, kv):
    vmem = pl.BlockSpec(memory_space=pltpu.VMEM)
    return pl.pallas_call(
        attend_kernel,
        out_shape=jax.ShapeDtypeStruct((ROWS, 4096), BF16),
        in_specs=[pl.BlockSpec(memory_space=pltpu.SMEM), vmem, vmem],
        out_specs=vmem,
        compiler_params=pltpu.CompilerParams(vmem_limit_bytes=48 << 20),
        cost_estimate=pl.CostEstimate(
            flops=4 << 30, bytes_accessed=10 << 20, transcendentals=8 << 20
        ),
        name="attend",
    )(limits, q, kv)


def body(
    queries, cache_keys, cache_values, ssm_input, input_map, output_map, log_decay, skip_gain,
    lengths, page_owner,
):
    rep_count = lax.axis_size("rep")
    my_index = lax.axis_index("ctx")
    length = lengths[0]
    key_rows = cache_keys[0]
    value_rows = cache_values[0]
    kv_width = key_rows.shape[1]
    first = my_index * ROWS

    both = jnp.concatenate([key_rows, value_rows], axis=1)
    gathered = lax.all_gather(both, "ctx", axis=0, tiled=True)

    live = (first < length).astype(F32)
    cum = jnp.cumsum(log_decay[0] * live, axis=0)
    cumt = jnp.transpose(cum)
    last = cumt[:, -1:]
    ef = (jnp.exp(last - cumt) * live).reshape(GR, HG, ROWS)
    wg = jnp.broadcast_to(jnp.exp(last), (128, 128)).reshape(GR, HG, 128)
    cumg = jnp.transpose(cum.reshape(ROWS, GR, HG), (1, 0, 2))
    ecum = jnp.transpose(jnp.exp(cum).reshape(ROWS, GR, 8, 4), (1, 2, 0, 3))
    skip = jnp.broadcast_to(jnp.repeat(skip_gain, MP)[None], (8, GR * GW))
    ssm_rows, pool = ssm_call(
        ssm_input[0], input_map[0], output_map[0], ef, cumt.reshape(GR, HG, ROWS), cumg, ecum,
        wg, jnp.broadcast_to(live, (8, 128)), skip,
    )

    page_rows = ROWS // PAGE
    stacked = jnp.stack(
        [
            key_rows.reshape(page_rows, PAGE, kv_width),
            value_rows.reshape(page_rows, PAGE, kv_width),
        ],
        axis=1,
    )
    page_number = my_index * page_rows + jnp.arange(page_rows, dtype=jnp.int32)
    alive_page = page_number * PAGE < length
    owners = page_owner[0, :, 0]
    onehot = (owners[:, None] == jnp.arange(rep_count, dtype=jnp.int32)[None, :]).astype(jnp.int32)
    ranking = jnp.cumsum(onehot, axis=0) - onehot
    slot_index = jnp.sum(ranking * onehot, axis=1)
    selector = jnp.transpose(onehot)[:, None, :] * (
        slot_index[None, None, :] == jnp.arange(CAP, dtype=jnp.int32)[None, :, None]
    ).astype(jnp.int32)
    selector = selector * alive_page.astype(jnp.int32)[None, None, :]
    buffer = jnp.einsum(
        "oqp,px->oqx",
        selector.astype(BF16),
        stacked.reshape(page_rows, 2 * PAGE * kv_width),
        preferred_element_type=F32,
    ).astype(BF16)
    buffer = buffer.reshape(rep_count, CAP, 2, PAGE, kv_width)
    page_ids = jnp.sum(selector * (page_number + 1)[None, None, :], axis=2) - 1
    got_pages = lax.all_to_all(buffer, "rep", split_axis=0, concat_axis=0, tiled=True)
    got_ids = lax.all_to_all(page_ids, "rep", split_axis=0, concat_axis=0, tiled=True)

    limits = jnp.stack([first, length]).astype(jnp.int32)
    attention_rows = attend_call(limits, queries[0], gathered)
    return (
        attention_rows[None],
        ssm_rows[None],
        pool[None],
        got_pages[None, None],
        got_ids[None, None],
    )


def solution(mesh):
    rows = P("rep", "ctx", None)
    return jax.shard_map(
        body,
        mesh=mesh,
        in_specs=(rows, rows, rows, rows, rows, rows, rows, P(), P("rep"), rows),
        out_specs=(
            rows,
            rows,
            P("ctx", None, "rep", None, None),
            P("ctx", "rep", None, None, None, None, None),
            P("ctx", "rep", None, None),
        ),
        check_vma=False,
    )
```

time: 1330 us -> 220 us (0.17)
  the two profiles are of different devices: /device:TPU:62 before, /device:TPU:29 now
where the time goes in v1:
time: 220 us
  Pallas kernels  171 us (78%)
  local copies, waits for them, and re-layouts  18.1 us (8%)
  between operations  14.8 us (7%)
  starting transfers between devices  10.9 us (5%)
  other arithmetic  4.07 us (2%)
    pallas_call x1, Pallas kernels, ssm_call(): pl.pallas_call(ssm_kernel, out_shape=(jax.ShapeDtypeStruct((ROWS, GR * GW...  130 us
    pallas_call x1, Pallas kernels, attend_call(): pl.pallas_call(attend_kernel, out_shape=jax.ShapeDtypeStruct((ROWS, 4096)...  41.6 us
    unnamed x15, local copies, waits for them, and re-layouts  6.29 us
    all_to_all x1, starting transfers between devices, body(): lax.all_to_all(page_ids, 'rep', split_axis=0, concat_axis=0, tiled=True)  5.98 us
    all_to_all x1, starting transfers between devices, body(): lax.all_to_all(buffer, 'rep', split_axis=0, concat_axis=0, tiled=True)  4.92 us
  transfers between devices with their start and end apart: 3, of which 0 were waited for; matrix products, arithmetic and copies ran while one was open for 7% of the time, Pallas kernels for 59%

profile of v1, /device:TPU:29, one launch (start us, length us, event | category | flops | bytes accessed | tf_op | source)
XLA Modules:
  0.0 219.9 jit_solution(16288541821150311400)
XLA Ops:
  7.2 1.9 pad_maximum_fusion
  9.8 0.8 fusion.6
  10.6 0.8 select_reduce_fusion
  11.5 0.2 multiply_reduce_fusion
  11.7 0.7 copy.49
  12.3 6.0 %all-to-all-start.1 = ((s32[8,1,4]{2,1,0:T(1,128)}), s32[8,1,4]{2,1,0:T(1,128)S(1)}, u32[]{:S(2)}, u32[]{:S(2)}) async-start(s32[8,1,4]{2,1,0:T(1,128)} %copy.49), calls=%async_computation.1 | async-start | bytes 8192 | tf_op jit(solution)/shard_map/all_to_all | solution.py:463
  18.3 1.1 copy.47
  19.4 0.2 copy.46
  19.6 0.7 convolution_convert_fusion
  20.3 2.5 %copy.48 = bf16[8,4,2,16,1024]{4,3,2,1,0:T(8,128)(2,1)} copy(bf16[8,4,2,16,1024]{4,0,3,2,1:T(8,128)(2,1)S(1)} %bitcast.40) | data formatting | bytes 4194304 | tf_op jit(solution)/shard_map/reshape | solution.py:460
  22.8 4.9 %all-to-all-start = ((bf16[8,4,2,16,1024]{4,3,2,1,0:T(8,128)(2,1)}), bf16[8,4,2,16,1024]{4,3,2,1,0:T(8,128)(2,1)S(1)}, u32[]{:S(2)}, u32[]{:S(2)}) async-start(bf16[8,4,2,16,1024]{4,3,2,1,0:T(8,128)(2,1)} %copy.48), calls=%async_computation | async-start | bytes 4194304 | tf_op jit(solution)/shard_map/all_to_all | solution.py:462
  27.7 0.2 reduce_window_sum.22
  27.9 0.1 copy.42
  28.0 0.7 copy.41
  28.8 0.7 copy.40
  29.5 0.8 copy.43
  30.4 0.1 copy.44
  30.5 2.0 copy.45
  32.4 0.1 broadcast_in_dim.42
  32.5 0.1 broadcast_in_dim.45
  32.6 0.1 broadcast_in_dim.46
  32.7 0.7 broadcast_in_dim.43.wg_ref
  33.4 0.6 broadcast_in_dim.44.live_ref
  34.0 0.7 broadcast_in_dim.47.skip_ref
  34.7 129.7 %ssm_exchange.1 = (bf16[128,8192]{1,0:T(8,128)(2,1)}, bf16[8,16,64,256]{3,2,1,0:T(8,128)(2,1)}) custom-call(bf16[128,8192]{1,0:T(8,128)(2,1)} %bitcast.43, bf16[128,1024]{1,0:T(8,128)(2,1)} %bitcast.54, bf16[128,1024]{1,0:T(8,128)(2,1)} %bitcast.55, f32[4,32,128]{2,1,0:T(8,128)} %bitcast.53, f32[4,32,128]{2,1,0:T(8,128)} %bitcast.52, ...), custom_call_target="tpu_custom_call" | custom-call | tf_op jit(solution)/shard_map/ssm_exchange/pallas_call | solution.py:311
  164.5 0.1 pad_add_fusion.limits
  164.5 0.7 copy.50
  165.2 41.6 %attend.1 = bf16[128,4096]{1,0:T(8,128)(2,1)} custom-call(s32[2]{0:T(128)S(1)} %pad_add_fusion.limits, bf16[128,4096]{1,0:T(8,128)(2,1)S(1)} %bitcast.37, bf16[2048,2048]{1,0:T(8,128)(2,1)} %all-gather.2.cloned.1.call-done.kv_ref), custom_call_target="tpu_custom_call" | custom-call | flops 4294967296 | bytes 10485760 | tf_op jit(solution)/shard_map/attend/pallas_call | solution.py:394
  206.8 1.3 copy.55
  208.1 1.6 copy-done.1
  209.7 2.0 copy.56
  211.7 1.3 copy.57
  (26 shorter events, 0.3 us)
Async XLA Ops:
  7.2 12.2 %copy-start.3 = (bf16[1,128,1024]{2,1,0:T(8,128)(2,1)S(1)}, bf16[1,128,1024]{2,1,0:T(8,128)(2,1)}, u32[]{:S(2)}) copy-start(bf16[1,128,1024]{2,1,0:T(8,128)(2,1)} %param.11) | copy-start | bytes 786436
  7.2 158.0 %all-gather.2.cloned.1.call-start = ((), (), s32[]{:S(2)}) async-start(), calls=%async_computation.2 | async-start | bytes 8912896 | tf_op jit(solution)/shard_map/all_gather | solution.py:420
  12.3 10.5 %all-to-all-start.1 = ((s32[8,1,4]{2,1,0:T(1,128)}), s32[8,1,4]{2,1,0:T(1,128)S(1)}, u32[]{:S(2)}, u32[]{:S(2)}) async-start(s32[8,1,4]{2,1,0:T(1,128)} %copy.49), calls=%async_computation.1 | async-start | bytes 8192 | tf_op jit(solution)/shard_map/all_to_all | solution.py:463
  22.8 4.9 %copy-start.4 = (f32[1,128,128]{2,1,0:T(8,128)S(1)}, f32[1,128,128]{2,1,0:T(8,128)}, u32[]{:S(2)}) copy-start(f32[1,128,128]{2,1,0:T(8,128)} %param.16) | copy-start | bytes 196612
  22.8 142.4 %all-to-all-start = ((bf16[8,4,2,16,1024]{4,3,2,1,0:T(8,128)(2,1)}), bf16[8,4,2,16,1024]{4,3,2,1,0:T(8,128)(2,1)S(1)}, u32[]{:S(2)}, u32[]{:S(2)}) async-start(bf16[8,4,2,16,1024]{4,3,2,1,0:T(8,128)(2,1)} %copy.48), calls=%async_computation | async-start | bytes 4194304 | tf_op jit(solution)/shard_map/all_to_all | solution.py:462
  27.7 4.8 %copy-start.5 = (f32[128]{0:T(128)S(1)}, f32[128]{0:T(128)}, u32[]{:S(2)}) copy-start(f32[128]{0:T(128)} %param.17) | copy-start | bytes 1540
  34.7 130.5 %copy-start = (bf16[1,128,4096]{2,1,0:T(8,128)(2,1)S(1)}, bf16[1,128,4096]{2,1,0:T(8,128)(2,1)}, u32[]{:S(2)}) copy-start(bf16[1,128,4096]{2,1,0:T(8,128)(2,1)} %param.10) | copy-start | bytes 3145732
  165.2 41.6 %copy-start.2 = (bf16[128,8192]{1,0:T(8,128)(2,1)S(1)}, bf16[128,8192]{1,0:T(8,128)(2,1)}, u32[]{:S(2)}) copy-start(bf16[128,8192]{1,0:T(8,128)(2,1)} %get-tuple-element.7) | copy-start | bytes 6291460
  206.8 2.9 %copy-start.1 = (bf16[8,16,64,256]{3,2,1,0:T(8,128)(2,1)S(1)}, bf16[8,16,64,256]{3,2,1,0:T(8,128)(2,1)}, u32[]{:S(2)}) copy-start(bf16[8,16,64,256]{3,2,1,0:T(8,128)(2,1)} %get-tuple-element.8) | copy-start | bytes 12582916
Sparse Core Ops, SparseCore 0:
  10.7 92.9 all-gather.1

commit v2 on v1

v2 whole, which is shorter than its diff:
```python
import math

import jax
import jax.numpy as jnp
from jax import lax
from jax.experimental import pallas as pl
from jax.experimental.pallas import tpu as pltpu
from jax.sharding import PartitionSpec as P

HD = 128
GR = 4
PAGE = 16
CAP = 4
MP = 64
NS = 256
ROWS = 128
HG = 32
GW = HG * MP
HALF = GW // 2
MESH = pl.DeviceIdType.MESH
F32 = jnp.float32
BF16 = jnp.bfloat16
ORDER = (1, 3, 2)


def mod4(v):
    return lax.rem(v + 8, 4)


def chunk_rows(piece):
    return pl.ds(pl.multiple_of(piece * 256, 256), 256)


def widen(rows):
    heads = rows.shape[0]
    both = jnp.concatenate([rows, rows], axis=1)
    return jnp.broadcast_to(both[:, None, :], (heads, MP, NS)).reshape(heads * MP, NS)


def pair_kernel(
    meta, q_ref, k_ref, v_ref, x_hbm, b_ref, c_ref, decay_ref, skip_ref,
    attn_ref, out_ref, pool_ref, pages_ref, ids_ref,
    x_ref, ef, cumt, cumg, ecum, wg, ft, ft_in, b_in, w_in, part, wprod, t_out, t_in, w4_in,
    e0_out, e0_in, e_out, e_in, inner, snap, q_in, kv_in, a_out, page_buf, id_buf,
    l_x, l_q, l_a, l_p, l_g, l_i,
    s_k, r_k, s_v, r_v, s_q, r_q, s_kv, r_kv, s_a, r_a, s_g, r_g, s_i, r_i,
    s_ft, r_ft, s_b, r_b, s_w, r_w, s_t, r_t, s_w4, r_w4, s_e0, r_e0, s_e, r_e, s_p, r_p,
):
    ctx = lax.axis_index("ctx")
    rep = lax.axis_index("rep")
    mx = lax.rem(ctx, 4)
    my = ctx // 4
    mz = rep // 2
    first = ctx * ROWS
    length = meta[0]

    def row_peer(j):
        return (my * 4 + j, rep)

    def col_peer(j):
        return (j * 4 + mx, rep)

    def remote(src, dst, send, recv, device):
        return pltpu.make_async_remote_copy(
            src_ref=src, dst_ref=dst, send_sem=send, recv_sem=recv, device_id=device,
            device_id_type=MESH,
        )

    local_x = pltpu.make_async_copy(x_hbm, x_ref, l_x)
    local_x.start()
    barrier = pltpu.get_barrier_semaphore()
    for i in range(1, 4):
        pl.semaphore_signal(barrier, inc=1, device_id=row_peer(mod4(mx + i)), device_id_type=MESH)
        pl.semaphore_signal(barrier, inc=1, device_id=col_peer(mod4(my + i)), device_id_type=MESH)
    for i in range(1, 8):
        pl.semaphore_signal(
            barrier, inc=1, device_id=(ctx, lax.rem(rep + i, 8)), device_id_type=MESH
        )

    lane = lax.broadcasted_iota(jnp.int32, (ROWS, 128), 1)
    line = lax.broadcasted_iota(jnp.int32, (ROWS, 128), 0)
    causal = lane <= line
    low = lane < MP
    live = jnp.where(jnp.full((1, 128), first, jnp.int32) < length, 1.0, 0.0)

    cum = jnp.dot(
        jnp.where(causal, 1.0, 0.0), decay_ref[...] * live,
        precision=lax.Precision.HIGHEST, preferred_element_type=F32,
    )
    turned = jnp.transpose(cum)
    last = turned[:, 127:128]
    ef[...] = (jnp.exp(last - turned) * live).reshape(GR, HG, ROWS)
    cumt[...] = turned.reshape(GR, HG, ROWS)
    wg[...] = jnp.broadcast_to(jnp.exp(last), (128, 128)).reshape(GR, HG, 128)
    grown = jnp.exp(cum)
    for g in range(GR):
        cumg[g] = cum[:, g * HG : (g + 1) * HG]
        for p in range(8):
            ecum[g, p] = grown[:, g * HG + p * 4 : g * HG + p * 4 + 4]

    pl.semaphore_wait(barrier, 13)
    sent = []

    def go(copy):
        copy.start()
        sent.append(copy)

    for i in ORDER:
        j = mod4(my + i)
        lanes = pl.ds(pl.multiple_of(j * 256, 256), 256)
        go(remote(k_ref.at[:, lanes], kv_in.at[my, mx, :, pl.ds(0, 256)], s_k.at[i], r_k.at[my],
                  col_peer(j)))
        go(remote(v_ref.at[:, lanes], kv_in.at[my, mx, :, pl.ds(256, 256)], s_v.at[i], r_v.at[my],
                  col_peer(j)))
    for i in ORDER:
        j = mod4(my + i)
        lanes = pl.ds(pl.multiple_of(j * 1024, 1024), 1024)
        go(remote(q_ref.at[:, lanes], q_in.at[my], s_q.at[i], r_q.at[my], col_peer(j)))
    own = pl.ds(pl.multiple_of(my * 256, 256), 256)
    kv_in[my, mx, :, 0:256] = k_ref[:, own]
    kv_in[my, mx, :, 256:512] = v_ref[:, own]
    local_q = pltpu.make_async_copy(
        q_ref.at[:, pl.ds(pl.multiple_of(my * 1024, 1024), 1024)], q_in.at[my], l_q
    )
    local_q.start()
    local_x.wait()

    def fade(j, u):
        def tile(t, carry):
            d = t // 2
            p = lax.rem(t, 2)
            lanes = pl.ds(pl.multiple_of(j * GW + d * 512 + u * 256 + p * 128, 128), 128)
            values = jnp.transpose(x_ref[:, lanes].astype(F32))
            factor = jnp.broadcast_to(
                ef[j, pl.ds(8 * d + 4 * u + 2 * p, 2), :][:, None, :], (2, MP, ROWS)
            ).reshape(128, ROWS)
            ft[j, u, pl.ds(pl.multiple_of(t * 128, 128), 128), :] = (values * factor).astype(BF16)
            return carry

        lax.fori_loop(0, 8, tile, 0, unroll=4)

    for u in range(2):
        for i in ORDER:
            j = mod4(mx + i)
            if u == 0:
                lanes = pl.ds(pl.multiple_of(j * NS, NS), NS)
                go(remote(b_ref.at[:, lanes], b_in.at[mx], s_b.at[i], r_b.at[mx], row_peer(j)))
                go(remote(wg.at[j], w_in.at[mx], s_w.at[i], r_w.at[mx], row_peer(j)))
            fade(j, u)
            go(remote(ft.at[j, u], ft_in.at[mx, u], s_ft.at[u, i], r_ft.at[u, mx], row_peer(j)))
        fade(mx, u)
        ft_in[mx, u] = ft[mx, u]
    b_in[mx] = b_ref[:, pl.ds(pl.multiple_of(mx * NS, NS), NS)]
    w_in[mx] = wg[mx]

    def fill_pages(o, carry):
        labels = []
        picks = []
        for e in range(CAP):
            label = meta[40 + o * CAP + e]
            labels.append(label)
            start = meta[8 + o * CAP + e] * PAGE
            hit = (lane[:PAGE] - line[:PAGE] == start) & (label >= 0)
            picks.append(jnp.where(hit, 1.0, 0.0))
        pick = jnp.concatenate(picks, axis=0).astype(BF16)
        for z, rows in enumerate((k_ref, v_ref)):
            taken = jnp.dot(pick, rows[...], preferred_element_type=F32).astype(BF16)
            page_buf[o, :, z] = taken.reshape(CAP, PAGE, 1024)
        spot = lax.broadcasted_iota(jnp.int32, (8, 128), 1)
        id_buf[o] = jnp.where(
            spot == 0, labels[0],
            jnp.where(spot == 1, labels[1], jnp.where(spot == 2, labels[2], labels[3])),
        )
        return carry

    lax.fori_loop(0, 8, fill_pages, 0)
    for i in range(1, 8):
        o = lax.rem(rep + i, 8)
        go(remote(page_buf.at[o], pages_ref.at[rep], s_g.at[i], r_g.at[rep], (ctx, o)))
        go(remote(id_buf.at[o], ids_ref.at[rep], s_i.at[i], r_i.at[rep], (ctx, o)))
    local_pages = pltpu.make_async_copy(page_buf.at[rep], pages_ref.at[rep], l_g)
    local_pages.start()
    local_ids = pltpu.make_async_copy(id_buf.at[rep], ids_ref.at[rep], l_i)
    local_ids.start()

    def inner_group(g, carry):
        lanes = pl.ds(pl.multiple_of(g * NS, NS), NS)
        products = lax.dot_general(
            c_ref[:, lanes], b_ref[:, lanes], (((1,), (1,)), ((), ())),
            preferred_element_type=F32,
        )
        products = jnp.where(causal, products * live, 0.0)
        for p in range(HG // 2):
            at = pl.ds(pl.multiple_of(g * GW + p * 128, 128), 128)
            values = x_ref[:, at]
            halves = []
            for k in range(2):
                h = 2 * p + k
                column = cumg[g, :, h : h + 1]
                row = cumt[g, h : h + 1, :]
                mix = (products * jnp.exp(jnp.minimum(column - row, 0.0))).astype(BF16)
                halves.append(jnp.dot(mix, values, preferred_element_type=F32))
            inner[:, at] = jnp.where(low, halves[0], halves[1]) + skip_ref[0:1, at] * (
                values.astype(F32) * live
            )
        return carry

    lax.fori_loop(0, GR, inner_group, 0)

    for i in ORDER:
        j = mod4(mx + i)
        remote(b_in.at[j], b_in.at[j], s_b.at[i], r_b.at[j], row_peer(j)).wait_recv()
        remote(w_in.at[j], w_in.at[j], s_w.at[i], r_w.at[j], row_peer(j)).wait_recv()

    running = w_in[0]
    for k in range(1, 4):
        wprod[k - 1] = running
        running = running * w_in[k]
    wprod[3] = running

    def scan_piece(u, piece):
        at = chunk_rows(piece)
        heads = pl.ds(piece * 8 + u * 4, 4)
        state = jnp.dot(ft_in[0, u, at, :], b_in[0], preferred_element_type=F32)
        for k in range(1, 4):
            part[k - 1, u, at, :] = state
            state = state * widen(w_in[k, heads, :]) + jnp.dot(
                ft_in[k, u, at, :], b_in[k], preferred_element_type=F32
            )
        t_out[u, at, :] = state.astype(BF16)

    for u in range(2):
        for i in ORDER:
            j = mod4(mx + i)
            remote(
                ft_in.at[j, u], ft_in.at[j, u], s_ft.at[u, i], r_ft.at[u, j], row_peer(j)
            ).wait_recv()
        for i in ORDER:
            j = mod4(my + i)
            scan_piece(u, j)
            if u == 0:
                heads = pl.ds(pl.multiple_of(j * 8, 8), 8)
                go(remote(wprod.at[3, heads, :], w4_in.at[my], s_w4.at[i], r_w4.at[my],
                          col_peer(j)))
            go(remote(t_out.at[u, chunk_rows(j), :], t_in.at[u, my], s_t.at[u, i], r_t.at[u, my],
                      col_peer(j)))
        scan_piece(u, my)
        t_in[u, my] = t_out[u, chunk_rows(my), :]
        if u == 0:
            w4_in[my] = wprod[3, pl.ds(pl.multiple_of(my * 8, 8), 8), :]
            for i in ORDER:
                j = mod4(my + i)
                for z, (send, recv) in enumerate(((s_k, r_k), (s_v, r_v))):
                    there = kv_in.at[j, mx, :, pl.ds(256 * z, 256)]
                    remote(there, there, send.at[i], recv.at[j], col_peer(j)).wait_recv()
            for i in ORDER:
                j = mod4(mx + i)
                go(remote(kv_in.at[:, mx], kv_in.at[:, mx], s_kv.at[i], r_kv.at[mx], row_peer(j)))

    for u in range(2):
        for i in ORDER:
            j = mod4(my + i)
            remote(t_in.at[u, j], t_in.at[u, j], s_t.at[u, i], r_t.at[u, j], col_peer(j)).wait_recv()
            if u == 0:
                remote(w4_in.at[j], w4_in.at[j], s_w4.at[i], r_w4.at[j], col_peer(j)).wait_recv()
        state = jnp.zeros((256, NS), F32)
        for k in range(4):
            e0_out[u, k] = state.astype(BF16)
            if k < 3:
                state = state * widen(w4_in[k, 4 * u : 4 * u + 4, :]) + t_in[u, k].astype(F32)
        for i in ORDER:
            j = mod4(my + i)
            go(remote(e0_out.at[u, j], e0_in.at[u, my], s_e0.at[u, i], r_e0.at[u, my], col_peer(j)))
        e0_in[u, my] = e0_out[u, my]

    for u in range(2):
        for d in (0, 1, 3, 2):
            piece = mod4(my + d)
            if d != 0:
                remote(
                    e0_in.at[u, piece], e0_in.at[u, piece], s_e0.at[u, d], r_e0.at[u, piece],
                    col_peer(piece),
                ).wait_recv()
            at = chunk_rows(piece)
            heads = pl.ds(piece * 8 + u * 4, 4)
            e_out[u, 0, at, :] = e0_in[u, piece]
            for k in range(1, 4):
                e_out[u, k, at, :] = (
                    e0_in[u, piece].astype(F32) * widen(wprod[k - 1, heads, :])
                    + part[k - 1, u, at, :]
                ).astype(BF16)
            for i in ORDER:
                j = mod4(mx + i)
                go(remote(e_out.at[u, j, at, :], e_in.at[u, mx, at, :], s_e.at[u, d, i],
                          r_e.at[u, mx, d], row_peer(j)))
            e_in[u, mx, at, :] = e_out[u, mx, at, :]

    for i in ORDER:
        j = mod4(mx + i)
        remote(kv_in.at[:, j], kv_in.at[:, j], s_kv.at[i], r_kv.at[j], row_peer(j)).wait_recv()
    local_q.wait()
    for i in ORDER:
        j = mod4(my + i)
        remote(q_in.at[j], q_in.at[j], s_q.at[i], r_q.at[j], col_peer(j)).wait_recv()

    scale = math.log2(math.e) / math.sqrt(HD)
    key_off = lax.broadcasted_iota(jnp.int32, (1, 512), 1)
    spread = lax.broadcasted_iota(jnp.int32, (ROWS, 512), 1) - lax.broadcasted_iota(
        jnp.int32, (ROWS, 512), 0
    )

    def attend(i, h):
        def two_heads(a, carry):
            wide = [
                pl.ds(pl.multiple_of((4 * h + 2 * a + r) * HD, HD), HD) for r in range(2)
            ]
            query = jnp.concatenate([q_in[i, :, wide[0]], q_in[i, :, wide[1]]], axis=0)
            scores = []
            for t in range(i + 1):
                keys = kv_in[t, :, :, h * HD : (h + 1) * HD].reshape(512, HD)
                raw = lax.dot_general(
                    query, keys, (((1,), (1,)), ((), ())), preferred_element_type=F32
                )
                if t > 0:
                    raw = raw + jnp.where(key_off + t * 512 < length, 0.0, -1e30)
                if t == i:
                    bias = jnp.where(spread <= mx * ROWS, 0.0, -1e30)
                    raw = raw + jnp.concatenate([bias, bias], axis=0)
                scores.append(raw)
            top = scores[0]
            for raw in scores[1:]:
                top = jnp.maximum(top, raw)
            top = jnp.max(top, axis=1, keepdims=True)
            total = None
            acc = None
            for t in range(i + 1):
                weights = jnp.exp2((scores[t] - top) * scale)
                values = kv_in[t, :, :, 256 + h * HD : 256 + (h + 1) * HD].reshape(512, HD)
                more = jnp.sum(weights, axis=1, keepdims=True)
                term = jnp.dot(weights.astype(BF16), values, preferred_element_type=F32)
                total = more if total is None else total + more
                acc = term if acc is None else acc + term
            result = (acc / total).astype(BF16)
            for r in range(2):
                a_out[i, :, wide[r]] = result[r * ROWS : (r + 1) * ROWS]
            return carry

        lax.fori_loop(0, 2, two_heads, 0)

    def a_copies(i):
        target = attn_ref.at[:, pl.ds(pl.multiple_of(my * 1024, 1024), 1024)]
        return (
            remote(a_out.at[i], target, s_a.at[i], r_a.at[my], col_peer(i)),
            pltpu.make_async_copy(a_out.at[i], target, l_a),
        )

    def snap_copies(u, d, s):
        piece = mod4(my + d)
        j = mod4(mx + mz + s)
        owner = 2 * j + piece // 2
        half = lax.rem(piece, 2)
        source = snap.at[j, pl.ds(piece * 8 + 4 * u, 4)]
        target = pool_ref.at[rep, pl.ds(half * 8 + 4 * u, 4)]
        return (
            owner,
            remote(source, target, s_p.at[u, d, s], r_p.at[rep, half, u], (ctx, owner)),
            pltpu.make_async_copy(source, target, l_p.at[half, u]),
        )

    units = [(3, 0), (3, 1), (2, 0), (2, 1), (1, 0), (1, 1), (0, 0), (0, 1)]
    for u in range(2):
        for d in (0, 1, 3, 2):
            piece = mod4(my + d)
            at = chunk_rows(piece)

            def finish(s, carry):
                j = mod4(mx + mz + s)

                @pl.when(j != mx)
                def _():
                    remote(
                        e_in.at[u, j, at, :], e_in.at[u, j, at, :], s_e.at[u, d, 1],
                        r_e.at[u, j, d], row_peer(j),
                    ).wait_recv()

                lanes = pl.ds(pl.multiple_of(j * NS, NS), NS)
                entering = e_in[u, j, at, :]
                mine = jnp.dot(ft[j, u, at, :], b_ref[:, lanes], preferred_element_type=F32)
                factor = widen(wg[j, pl.ds(piece * 8 + u * 4, 4), :])
                leaving = (mine + factor * entering.astype(F32)).astype(BF16)
                snap[j, pl.ds(piece * 8 + u * 4, 4)] = leaving.reshape(4, MP, NS)
                owner, away, here = snap_copies(u, d, s)

                @pl.when(owner != rep)
                def _():
                    away.start()

                @pl.when(owner == rep)
                def _():
                    here.start()

                carried = lax.dot_general(
                    c_ref[:, lanes], entering, (((1,), (1,)), ((), ())),
                    preferred_element_type=F32,
                )
                for p in range(2):
                    scales = [
                        jnp.broadcast_to(
                            ecum[j, piece * 2 + u, :, 2 * p + k : 2 * p + k + 1], (ROWS, 128)
                        )
                        for k in range(2)
                    ]
                    wide = pl.ds(
                        pl.multiple_of(j * GW + piece * 512 + u * 256 + p * 128, 128), 128
                    )
                    out_ref[:, wide] = (
                        inner[:, wide]
                        + jnp.where(low, scales[0], scales[1]) * carried[:, p * 128 : p * 128 + 128]
                    ).astype(BF16)
                return carry

            lax.fori_loop(0, 4, finish, 0)
            i, h = units.pop(0)
            attend(i, h)
            if h == 1:
                away, here = a_copies(i)
                pl.when(i != my)(away.start)
                pl.when(i == my)(here.start)

    for c in sent:
        c.wait_send()
    for i in range(4):
        away, here = a_copies(i)
        pl.when(i != my)(away.wait_send)
        pl.when(i == my)(here.wait)
    for u in range(2):
        for d in range(4):

            def drain(s, carry):
                owner, away, here = snap_copies(u, d, s)
                pl.when(owner != rep)(away.wait_send)
                pl.when(owner == rep)(here.wait)
                return carry

            lax.fori_loop(0, 4, drain, 0)
    local_pages.wait()
    local_ids.wait()
    for i in ORDER:
        j = mod4(my + i)
        there = attn_ref.at[:, pl.ds(pl.multiple_of(j * 1024, 1024), 1024)]
        remote(there, there, s_a.at[i], r_a.at[j], col_peer(j)).wait_recv()
    for i in range(1, 8):
        o = lax.rem(rep + i, 8)
        remote(pages_ref.at[o], pages_ref.at[o], s_g.at[i], r_g.at[o], (ctx, o)).wait_recv()
        remote(ids_ref.at[o], ids_ref.at[o], s_i.at[i], r_i.at[o], (ctx, o)).wait_recv()
        for half in range(2):
            for u in range(2):
                there = pool_ref.at[o, pl.ds(half * 8 + 4 * u, 4)]
                remote(there, there, s_p.at[0, 0, 0], r_p.at[o, half, u], (ctx, o)).wait_recv()


def pair_call(meta, q, k, v, x, b, c, decay, skip):
    def dma(*shape):
        return pltpu.SemaphoreType.DMA(shape)

    vmem = pl.BlockSpec(memory_space=pltpu.VMEM)
    far = pl.BlockSpec(memory_space=pl.ANY)
    return pl.pallas_call(
        pair_kernel,
        out_shape=(
            jax.ShapeDtypeStruct((ROWS, 4096), BF16),
            jax.ShapeDtypeStruct((ROWS, GR * GW), BF16),
            jax.ShapeDtypeStruct((8, 16, MP, NS), BF16),
            jax.ShapeDtypeStruct((8, CAP, 2, PAGE, 1024), BF16),
            jax.ShapeDtypeStruct((8, 8, 128), jnp.int32),
        ),
        in_specs=[
            pl.BlockSpec(memory_space=pltpu.SMEM), far, vmem, vmem, far, vmem, vmem, vmem, vmem
        ],
        out_specs=(far, vmem, far, far, far),
        scratch_shapes=[
            pltpu.VMEM((ROWS, GR * GW), BF16),
            pltpu.VMEM((GR, HG, ROWS), F32),
            pltpu.VMEM((GR, HG, ROWS), F32),
            pltpu.VMEM((GR, ROWS, HG), F32),
            pltpu.VMEM((GR, 8, ROWS, 4), F32),
            pltpu.VMEM((GR, HG, 128), F32),
            pltpu.VMEM((4, 2, HALF, ROWS), BF16),
            pltpu.VMEM((4, 2, HALF, ROWS), BF16),
            pltpu.VMEM((4, ROWS, NS), BF16),
            pltpu.VMEM((4, HG, 128), F32),
            pltpu.VMEM((3, 2, HALF, NS), F32),
            pltpu.VMEM((4, HG, 128), F32),
            pltpu.VMEM((2, HALF, NS), BF16),
            pltpu.VMEM((2, 4, 256, NS), BF16),
            pltpu.VMEM((4, 8, 128), F32),
            pltpu.VMEM((2, 4, 256, NS), BF16),
            pltpu.VMEM((2, 4, 256, NS), BF16),
            pltpu.VMEM((2, 4, HALF, NS), BF16),
            pltpu.VMEM((2, 4, HALF, NS), BF16),
            pltpu.VMEM((ROWS, GR * GW), F32),
            pltpu.VMEM((4, HG, MP, NS), BF16),
            pltpu.VMEM((4, ROWS, 1024), BF16),
            pltpu.VMEM((4, 4, ROWS, 512), BF16),
            pltpu.VMEM((4, ROWS, 1024), BF16),
            pltpu.VMEM((8, CAP, 2, PAGE, 1024), BF16),
            pltpu.VMEM((8, 8, 128), jnp.int32),
            pltpu.SemaphoreType.DMA, pltpu.SemaphoreType.DMA, pltpu.SemaphoreType.DMA,
            dma(2, 2), pltpu.SemaphoreType.DMA, pltpu.SemaphoreType.DMA,
            dma(4), dma(4), dma(4), dma(4), dma(4), dma(4), dma(4), dma(4), dma(4), dma(4),
            dma(8), dma(8), dma(8), dma(8),
            dma(2, 4), dma(2, 4), dma(4), dma(4), dma(4), dma(4),
            dma(2, 4), dma(2, 4), dma(4), dma(4), dma(2, 4), dma(2, 4),
            dma(2, 4, 4), dma(2, 4, 4), dma(2, 4, 4), dma(8, 2, 2),
        ],
        compiler_params=pltpu.CompilerParams(
            collective_id=0, has_side_effects=True, vmem_limit_bytes=60 << 20
        ),
        name="layer_pair",
    )(meta, q, k, v, x, b, c, decay, skip)


def body(
    queries, cache_keys, cache_values, ssm_input, input_map, output_map, log_decay, skip_gain,
    lengths, page_owner,
):
    page_rows = ROWS // PAGE
    page_number = lax.axis_index("ctx") * page_rows + jnp.arange(page_rows, dtype=jnp.int32)
    alive_page = page_number * PAGE < lengths[0]
    owners = page_owner[0, :, 0]
    same = (owners[:, None] == owners[None, :]) & (
        jnp.arange(page_rows)[None, :] < jnp.arange(page_rows)[:, None]
    )
    slot = jnp.sum(same.astype(jnp.int32), axis=1)
    place = owners * CAP + slot
    chosen = (
        (jnp.arange(8 * CAP, dtype=jnp.int32)[:, None] == place[None, :]) & alive_page[None, :]
    ).astype(jnp.int32)
    index = jnp.sum(chosen * jnp.arange(page_rows, dtype=jnp.int32)[None, :], axis=1)
    label = jnp.sum(chosen * (page_number + 1)[None, :], axis=1) - 1
    meta = jnp.concatenate([jnp.broadcast_to(lengths, (8,)), index, label]).astype(jnp.int32)
    skip = jnp.repeat(skip_gain, MP)[None]
    attention, rows, pool, pages, ids = pair_call(
        meta, queries[0], cache_keys[0], cache_values[0], ssm_input[0], input_map[0],
        output_map[0], log_decay[0], skip,
    )
    return (
        attention[None], rows[None], pool[None], pages[None, None], ids[None, None, :, 0, :CAP]
    )


def solution(mesh):
    rows = P("rep", "ctx", None)
    return jax.shard_map(
        body,
        mesh=mesh,
        in_specs=(rows, rows, rows, rows, rows, rows, rows, P(), P("rep"), rows),
        out_specs=(
            rows,
            rows,
            P("ctx", None, "rep", None, None),
            P("ctx", "rep", None, None, None, None, None),
            P("ctx", "rep", None, None),
        ),
        check_vma=False,
    )
```

time: 220 us -> 141 us (0.64)
  the two profiles are of different devices: /device:TPU:29 before, /device:TPU:7 now
where the time goes in v2:
time: 141 us; the launch traced here: 138 us
  Pallas kernels  122 us (87%)
  local copies, waits for them, and re-layouts  12.7 us (9%)
  other arithmetic  2.27 us (2%)
    pallas_call x1, Pallas kernels, pair_call(): pl.pallas_call(pair_kernel, out_shape=(jax.ShapeDtypeStruct((ROWS, 4096),...  122 us
    unnamed x10, local copies, waits for them, and re-layouts  9.66 us

profile of v2, /device:TPU:7, one launch (start us, length us, event | category | flops | bytes accessed | tf_op | source)
XLA Modules:
  0.0 138.5 jit_solution(1768013598369883676)
XLA Ops:
  1.3 0.9 convert_reduce_fusion
  2.2 0.7 fusion.2
  2.9 0.1 select_reduce_fusion.1
  3.0 0.6 pad_add_fusion.meta
  3.6 0.7 broadcast_in_dim.31
  4.3 0.7 broadcast_in_dim_reshape.3.skip_ref
  5.0 122.2 %layer_pair.1 = (bf16[128,4096]{1,0:T(8,128)(2,1)}, bf16[128,8192]{1,0:T(8,128)(2,1)}, bf16[8,16,64,256]{3,2,1,0:T(8,128)(2,1)}, bf16[8,4,2,16,1024]{4,3,2,1,0:T(8,128)(2,1)}, s32[8,8,128]{2,1,0:T(8,128)}) custom-call(s32[72]{0:T(128)} %pad_add_fusion.meta, bf16[128,4096]{1,0:T(8,128)(2,1)} %bitcast.21, bf16[128,1024]{1,0:T(8,128)(2,1)} %bitcast.23, ...), custom_call_target="tpu_custom_call" | custom-call | tf_op jit(solution)/shard_map/layer_pair/pallas_call | solution.py:468
  127.2 0.0 copy-start.2
  127.3 0.9 slice.3
  128.2 0.7 copy.17
  128.8 2.3 %copy.23 = bf16[1,128,4096]{2,1,0:T(8,128)(2,1)} copy(bf16[1,128,4096]{2,1,0:T(8,128)(2,1)} %bitcast.22) | data formatting | bytes 2097152
  131.1 0.0 copy-done.2
  131.1 0.0 copy-start
  131.1 1.3 copy.24
  132.4 1.6 %copy-done = bf16[8,16,64,256]{3,2,1,0:T(8,128)(2,1)S(1)} copy-done((bf16[8,16,64,256]{3,2,1,0:T(8,128)(2,1)S(1)}, bf16[8,16,64,256]{3,2,1,0:T(8,128)(2,1)}, u32[]{:S(2)}) %copy-start) | copy-done | bytes 4194328
  134.1 0.0 copy-start.1
  134.1 2.1 %copy.25 = bf16[1,8,16,64,256]{4,3,2,1,0:T(8,128)(2,1)} copy(bf16[1,8,16,64,256]{4,3,2,1,0:T(8,128)(2,1)S(1)} %bitcast.17) | data formatting | bytes 8388608
  136.2 1.0 copy-done.1
  137.2 1.3 copy.26
  (3 shorter events, 0.0 us)
Async XLA Ops:
  127.2 3.9 %copy-start.2 = (bf16[128,8192]{1,0:T(8,128)(2,1)S(1)}, bf16[128,8192]{1,0:T(8,128)(2,1)}, u32[]{:S(2)}) copy-start(bf16[128,8192]{1,0:T(8,128)(2,1)} %get-tuple-element.11) | copy-start | bytes 6291460
  131.1 2.9 %copy-start = (bf16[8,16,64,256]{3,2,1,0:T(8,128)(2,1)S(1)}, bf16[8,16,64,256]{3,2,1,0:T(8,128)(2,1)}, u32[]{:S(2)}) copy-start(bf16[8,16,64,256]{3,2,1,0:T(8,128)(2,1)} %get-tuple-element.12) | copy-start | bytes 12582916
  134.1 3.1 %copy-start.1 = (bf16[8,4,2,16,1024]{4,3,2,1,0:T(8,128)(2,1)S(1)}, bf16[8,4,2,16,1024]{4,3,2,1,0:T(8,128)(2,1)}, u32[]{:S(2)}) copy-start(bf16[8,4,2,16,1024]{4,3,2,1,0:T(8,128)(2,1)} %get-tuple-element.13) | copy-start | bytes 6291460

commit v3 on v2

--- a/solution.py
+++ b/solution.py
@@ -38,12 +38,12 @@
 
 
 def pair_kernel(
-    meta, q_ref, k_ref, v_ref, x_hbm, b_ref, c_ref, decay_ref, skip_ref,
+    lengths, owners, gains, q_ref, k_hbm, v_hbm, x_hbm, b_hbm, c_hbm, decay_hbm,
     attn_ref, out_ref, pool_ref, pages_ref, ids_ref,
-    x_ref, ef, cumt, cumg, ecum, wg, ft, ft_in, b_in, w_in, part, wprod, t_out, t_in, w4_in,
+    k_ref, v_ref, x_ref, b_ref, c_ref, decay_ref, ef, cumt, cumg, ecum, wg, ft, ft_in, b_in, w_in, part, wprod, t_out, t_in, w4_in,
     e0_out, e0_in, e_out, e_in, inner, snap, q_in, kv_in, a_out, page_buf, id_buf,
-    l_x, l_q, l_a, l_p, l_g, l_i,
-    s_k, r_k, s_v, r_v, s_q, r_q, s_kv, r_kv, s_a, r_a, s_g, r_g, s_i, r_i,
+    l_in, l_q, l_a, l_p, l_g, l_i,
+    s_k, r_k, s_v, r_v, s_q, r_q, s_kv, r_kv, s_kw, r_kw, s_a, r_a, s_g, r_g, s_i, r_i,
     s_ft, r_ft, s_b, r_b, s_w, r_w, s_t, r_t, s_w4, r_w4, s_e0, r_e0, s_e, r_e, s_p, r_p,
 ):
     ctx = lax.axis_index("ctx")
@@ -52,7 +52,7 @@
     my = ctx // 4
     mz = rep // 2
     first = ctx * ROWS
-    length = meta[0]
+    length = lengths[0]
 
     def row_peer(j):
         return (my * 4 + j, rep)
@@ -66,8 +66,6 @@
             device_id_type=MESH,
         )
 
-    local_x = pltpu.make_async_copy(x_hbm, x_ref, l_x)
-    local_x.start()
     barrier = pltpu.get_barrier_semaphore()
     for i in range(1, 4):
         pl.semaphore_signal(barrier, inc=1, device_id=row_peer(mod4(mx + i)), device_id_type=MESH)
@@ -76,6 +74,15 @@
         pl.semaphore_signal(
             barrier, inc=1, device_id=(ctx, lax.rem(rep + i, 8)), device_id_type=MESH
         )
+    loads = [
+        pltpu.make_async_copy(src, dst, l_in.at[n])
+        for n, (src, dst) in enumerate((
+            (decay_hbm, decay_ref), (x_hbm, x_ref), (b_hbm, b_ref), (k_hbm, k_ref),
+            (v_hbm, v_ref), (c_hbm, c_ref),
+        ))
+    ]
+    for load in loads:
+        load.start()
 
     lane = lax.broadcasted_iota(jnp.int32, (ROWS, 128), 1)
     line = lax.broadcasted_iota(jnp.int32, (ROWS, 128), 0)
@@ -83,6 +90,7 @@
     low = lane < MP
     live = jnp.where(jnp.full((1, 128), first, jnp.int32) < length, 1.0, 0.0)
 
+    loads[0].wait()
     cum = jnp.dot(
         jnp.where(causal, 1.0, 0.0), decay_ref[...] * live,
         precision=lax.Precision.HIGHEST, preferred_element_type=F32,
@@ -105,26 +113,6 @@
         copy.start()
         sent.append(copy)
 
-    for i in ORDER:
-        j = mod4(my + i)
-        lanes = pl.ds(pl.multiple_of(j * 256, 256), 256)
-        go(remote(k_ref.at[:, lanes], kv_in.at[my, mx, :, pl.ds(0, 256)], s_k.at[i], r_k.at[my],
-                  col_peer(j)))
-        go(remote(v_ref.at[:, lanes], kv_in.at[my, mx, :, pl.ds(256, 256)], s_v.at[i], r_v.at[my],
-                  col_peer(j)))
-    for i in ORDER:
-        j = mod4(my + i)
-        lanes = pl.ds(pl.multiple_of(j * 1024, 1024), 1024)
-        go(remote(q_ref.at[:, lanes], q_in.at[my], s_q.at[i], r_q.at[my], col_peer(j)))
-    own = pl.ds(pl.multiple_of(my * 256, 256), 256)
-    kv_in[my, mx, :, 0:256] = k_ref[:, own]
-    kv_in[my, mx, :, 256:512] = v_ref[:, own]
-    local_q = pltpu.make_async_copy(
-        q_ref.at[:, pl.ds(pl.multiple_of(my * 1024, 1024), 1024)], q_in.at[my], l_q
-    )
-    local_q.start()
-    local_x.wait()
-
     def fade(j, u):
         def tile(t, carry):
             d = t // 2
@@ -139,6 +127,8 @@
 
         lax.fori_loop(0, 8, tile, 0, unroll=4)
 
+    loads[1].wait()
+    loads[2].wait()
     for u in range(2):
         for i in ORDER:
             j = mod4(mx + i)
@@ -148,20 +138,48 @@
                 go(remote(wg.at[j], w_in.at[mx], s_w.at[i], r_w.at[mx], row_peer(j)))
             fade(j, u)
             go(remote(ft.at[j, u], ft_in.at[mx, u], s_ft.at[u, i], r_ft.at[u, mx], row_peer(j)))
+        if u == 0:
+            loads[3].wait()
+            loads[4].wait()
+            for i in ORDER:
+                j = mod4(my + i)
+                lanes = pl.ds(pl.multiple_of(j * 256, 256), 256)
+                go(remote(k_ref.at[:, lanes], kv_in.at[my, mx, :, pl.ds(0, 256)], s_k.at[i], r_k.at[my],
+                          col_peer(j)))
+                go(remote(v_ref.at[:, lanes], kv_in.at[my, mx, :, pl.ds(256, 256)], s_v.at[i], r_v.at[my],
+                          col_peer(j)))
+            for i in ORDER:
+                j = mod4(my + i)
+                lanes = pl.ds(pl.multiple_of(j * 1024, 1024), 1024)
+                go(remote(q_ref.at[:, lanes], q_in.at[my], s_q.at[i], r_q.at[my], col_peer(j)))
+            own = pl.ds(pl.multiple_of(my * 256, 256), 256)
+            kv_in[my, mx, :, 0:256] = k_ref[:, own]
+            kv_in[my, mx, :, 256:512] = v_ref[:, own]
+            local_q = pltpu.make_async_copy(
+                q_ref.at[:, pl.ds(pl.multiple_of(my * 1024, 1024), 1024)], q_in.at[my], l_q
+            )
+            local_q.start()
         fade(mx, u)
         ft_in[mx, u] = ft[mx, u]
     b_in[mx] = b_ref[:, pl.ds(pl.multiple_of(mx * NS, NS), NS)]
     w_in[mx] = wg[mx]
 
+    places = []
+    for p in range(8):
+        slot = jnp.int32(0)
+        for r in range(p):
+            slot = slot + jnp.where(owners[r] == owners[p], 1, 0)
+        places.append(jnp.where(first < length, owners[p] * CAP + slot, -1))
+
     def fill_pages(o, carry):
         labels = []
         picks = []
         for e in range(CAP):
-            label = meta[40 + o * CAP + e]
-            labels.append(label)
-            start = meta[8 + o * CAP + e] * PAGE
-            hit = (lane[:PAGE] - line[:PAGE] == start) & (label >= 0)
-            picks.append(jnp.where(hit, 1.0, 0.0))
+            page = jnp.int32(-1000)
+            for p in range(8):
+                page = jnp.where(places[p] == o * CAP + e, p, page)
+            labels.append(jnp.where(page >= 0, page + ctx * 8, -1))
+            picks.append(jnp.where(lane[:PAGE] - line[:PAGE] == page * PAGE, 1.0, 0.0))
         pick = jnp.concatenate(picks, axis=0).astype(BF16)
         for z, rows in enumerate((k_ref, v_ref)):
             taken = jnp.dot(pick, rows[...], preferred_element_type=F32).astype(BF16)
@@ -182,6 +200,8 @@
     local_pages.start()
     local_ids = pltpu.make_async_copy(id_buf.at[rep], ids_ref.at[rep], l_i)
     local_ids.start()
+
+    loads[5].wait()
 
     def inner_group(g, carry):
         lanes = pl.ds(pl.multiple_of(g * NS, NS), NS)
@@ -200,9 +220,8 @@
                 row = cumt[g, h : h + 1, :]
                 mix = (products * jnp.exp(jnp.minimum(column - row, 0.0))).astype(BF16)
                 halves.append(jnp.dot(mix, values, preferred_element_type=F32))
-            inner[:, at] = jnp.where(low, halves[0], halves[1]) + skip_ref[0:1, at] * (
-                values.astype(F32) * live
-            )
+            gain = jnp.where(low[0:1], gains[g * HG + 2 * p], gains[g * HG + 2 * p + 1]) * live
+            inner[:, at] = jnp.where(low, halves[0], halves[1]) + gain * values.astype(F32)
         return carry
 
     lax.fori_loop(0, GR, inner_group, 0)
@@ -253,7 +272,7 @@
                 for z, (send, recv) in enumerate(((s_k, r_k), (s_v, r_v))):
                     there = kv_in.at[j, mx, :, pl.ds(256 * z, 256)]
                     remote(there, there, send.at[i], recv.at[j], col_peer(j)).wait_recv()
-            for i in ORDER:
+            for i in (1, 3):
                 j = mod4(mx + i)
                 go(remote(kv_in.at[:, mx], kv_in.at[:, mx], s_kv.at[i], r_kv.at[mx], row_peer(j)))
 
@@ -272,6 +291,12 @@
             j = mod4(my + i)
             go(remote(e0_out.at[u, j], e0_in.at[u, my], s_e0.at[u, i], r_e0.at[u, my], col_peer(j)))
         e0_in[u, my] = e0_out[u, my]
+
+    for n, i in enumerate((1, 3)):
+        j = mod4(mx - i)
+        remote(kv_in.at[:, j], kv_in.at[:, j], s_kv.at[i], r_kv.at[j], row_peer(j)).wait_recv()
+        there = kv_in.at[pl.ds(2 * n, 2), j]
+        go(remote(there, there, s_kw.at[n], r_kw.at[n], row_peer(mod4(mx + i))))
 
     for u in range(2):
         for d in (0, 1, 3, 2):
@@ -295,9 +320,9 @@
                           r_e.at[u, mx, d], row_peer(j)))
             e_in[u, mx, at, :] = e_out[u, mx, at, :]
 
-    for i in ORDER:
-        j = mod4(mx + i)
-        remote(kv_in.at[:, j], kv_in.at[:, j], s_kv.at[i], r_kv.at[j], row_peer(j)).wait_recv()
+    for n in range(2):
+        there = kv_in.at[pl.ds(2 * n, 2), mod4(mx + 2)]
+        remote(there, there, s_kw.at[n], r_kw.at[n], row_peer(mod4(mx + 1))).wait_recv()
     local_q.wait()
     for i in ORDER:
         j = mod4(my + i)
@@ -459,7 +484,7 @@
                 remote(there, there, s_p.at[0, 0, 0], r_p.at[o, half, u], (ctx, o)).wait_recv()
 
 
-def pair_call(meta, q, k, v, x, b, c, decay, skip):
+def pair_call(lengths, owners, gains, q, k, v, x, b, c, decay):
     def dma(*shape):
         return pltpu.SemaphoreType.DMA(shape)
 
@@ -474,12 +499,15 @@
             jax.ShapeDtypeStruct((8, CAP, 2, PAGE, 1024), BF16),
             jax.ShapeDtypeStruct((8, 8, 128), jnp.int32),
         ),
-        in_specs=[
-            pl.BlockSpec(memory_space=pltpu.SMEM), far, vmem, vmem, far, vmem, vmem, vmem, vmem
-        ],
+        in_specs=[pl.BlockSpec(memory_space=pltpu.SMEM)] * 3 + [far] * 7,
         out_specs=(far, vmem, far, far, far),
         scratch_shapes=[
+            pltpu.VMEM((ROWS, 1024), BF16),
+            pltpu.VMEM((ROWS, 1024), BF16),
             pltpu.VMEM((ROWS, GR * GW), BF16),
+            pltpu.VMEM((ROWS, 1024), BF16),
+            pltpu.VMEM((ROWS, 1024), BF16),
+            pltpu.VMEM((ROWS, 128), F32),
             pltpu.VMEM((GR, HG, ROWS), F32),
             pltpu.VMEM((GR, HG, ROWS), F32),
             pltpu.VMEM((GR, ROWS, HG), F32),
@@ -505,9 +533,10 @@
             pltpu.VMEM((4, ROWS, 1024), BF16),
             pltpu.VMEM((8, CAP, 2, PAGE, 1024), BF16),
             pltpu.VMEM((8, 8, 128), jnp.int32),
-            pltpu.SemaphoreType.DMA, pltpu.SemaphoreType.DMA, pltpu.SemaphoreType.DMA,
+            dma(6), pltpu.SemaphoreType.DMA, pltpu.SemaphoreType.DMA,
             dma(2, 2), pltpu.SemaphoreType.DMA, pltpu.SemaphoreType.DMA,
-            dma(4), dma(4), dma(4), dma(4), dma(4), dma(4), dma(4), dma(4), dma(4), dma(4),
+            dma(4), dma(4), dma(4), dma(4), dma(4), dma(4), dma(4), dma(4), dma(2), dma(2),
+            dma(4), dma(4),
             dma(8), dma(8), dma(8), dma(8),
             dma(2, 4), dma(2, 4), dma(4), dma(4), dma(4), dma(4),
             dma(2, 4), dma(2, 4), dma(4), dma(4), dma(2, 4), dma(2, 4),
@@ -517,35 +546,50 @@
             collective_id=0, has_side_effects=True, vmem_limit_bytes=60 << 20
         ),
         name="layer_pair",
-    )(meta, q, k, v, x, b, c, decay, skip)
+    )(lengths, owners, gains, q, k, v, x, b, c, decay)
+
+
+def place_kernel(a, b, c, d, ids, a_out, b_out, c_out, d_out, ids_out, sems):
+    copies = []
+    for src, dst, parts in ((c, c_out, 8), (b, b_out, 4), (d, d_out, 4), (a, a_out, 2)):
+        size = src.shape[0] // parts
+        for n in range(parts):
+            at = pl.ds(n * size, size)
+            copies.append(pltpu.make_async_copy(src.at[at], dst.at[at], sems.at[len(copies)]))
+    for copy in copies:
+        copy.start()
+    turned = jnp.transpose(ids[:, 0, :].astype(F32))
+    ids_out[...] = turned[:CAP].astype(jnp.int32)
+    for copy in copies:
+        copy.wait()
+
+
+def place_call(*arrays):
+    far = pl.BlockSpec(memory_space=pl.ANY)
+    vmem = pl.BlockSpec(memory_space=pltpu.VMEM)
+    shapes = [jax.ShapeDtypeStruct(x.shape, x.dtype) for x in arrays[:4]]
+    return pl.pallas_call(
+        place_kernel,
+        out_shape=(*shapes, jax.ShapeDtypeStruct((CAP, 8), jnp.int32)),
+        in_specs=[far] * 4 + [vmem],
+        out_specs=(far, far, far, far, vmem),
+        scratch_shapes=[pltpu.SemaphoreType.DMA((18,))],
+        compiler_params=pltpu.CompilerParams(vmem_limit_bytes=60 << 20),
+        name="place_outputs",
+    )(*arrays)
 
 
 def body(
     queries, cache_keys, cache_values, ssm_input, input_map, output_map, log_decay, skip_gain,
     lengths, page_owner,
 ):
-    page_rows = ROWS // PAGE
-    page_number = lax.axis_index("ctx") * page_rows + jnp.arange(page_rows, dtype=jnp.int32)
-    alive_page = page_number * PAGE < lengths[0]
-    owners = page_owner[0, :, 0]
-    same = (owners[:, None] == owners[None, :]) & (
-        jnp.arange(page_rows)[None, :] < jnp.arange(page_rows)[:, None]
+    results = pair_call(
+        lengths, page_owner.reshape(8), skip_gain, queries[0], cache_keys[0], cache_values[0],
+        ssm_input[0], input_map[0], output_map[0], log_decay[0],
     )
-    slot = jnp.sum(same.astype(jnp.int32), axis=1)
-    place = owners * CAP + slot
-    chosen = (
-        (jnp.arange(8 * CAP, dtype=jnp.int32)[:, None] == place[None, :]) & alive_page[None, :]
-    ).astype(jnp.int32)
-    index = jnp.sum(chosen * jnp.arange(page_rows, dtype=jnp.int32)[None, :], axis=1)
-    label = jnp.sum(chosen * (page_number + 1)[None, :], axis=1) - 1
-    meta = jnp.concatenate([jnp.broadcast_to(lengths, (8,)), index, label]).astype(jnp.int32)
-    skip = jnp.repeat(skip_gain, MP)[None]
-    attention, rows, pool, pages, ids = pair_call(
-        meta, queries[0], cache_keys[0], cache_values[0], ssm_input[0], input_map[0],
-        output_map[0], log_decay[0], skip,
-    )
+    attention, rows, pool, pages, ids = place_call(*results)
     return (
-        attention[None], rows[None], pool[None], pages[None, None], ids[None, None, :, 0, :CAP]
+        attention[None], rows[None], pool[None], pages[None, None], jnp.transpose(ids)[None, None]
     )
 
 

time: 141 us -> 408 us (2.89)
  Pallas kernels: 122 us -> 406 us
  local copies, waits for them, and re-layouts: 12.7 us -> 0 us
    pallas_call x0 -> x1, Pallas kernels: none -> 288 us  [place_call(): pl.pallas_call(place_kernel, out_shape=(*shapes, jax.ShapeDtypeStruct((CA...]
    unnamed x10 -> x0, local copies, waits for them, and re-layouts: 9.66 us -> none
    pallas_call x1, Pallas kernels: 122 us -> 117 us  [pair_call(): pl.pallas_call(pair_kernel, out_shape=(jax.ShapeDtypeStruct((ROWS, 4096),...]
where the time goes in v3:
time: 408 us; the launch traced here: 407 us
  Pallas kernels  406 us (100%)
    pallas_call x1, Pallas kernels, place_call(): pl.pallas_call(place_kernel, out_shape=(*shapes, jax.ShapeDtypeStruct((CA...  288 us
    pallas_call x1, Pallas kernels, pair_call(): pl.pallas_call(pair_kernel, out_shape=(jax.ShapeDtypeStruct((ROWS, 4096),...  117 us

profile of v3, /device:TPU:7, one launch (start us, length us, event | category | flops | bytes accessed | tf_op | source)
XLA Modules:
  0.0 406.8 jit_solution(1959760874344128099)
XLA Ops:
  1.3 117.1 %layer_pair.1 = (bf16[128,4096]{1,0:T(8,128)(2,1)}, bf16[128,8192]{1,0:T(8,128)(2,1)}, bf16[8,16,64,256]{3,2,1,0:T(8,128)(2,1)}, bf16[8,4,2,16,1024]{4,3,2,1,0:T(8,128)(2,1)}, s32[8,8,128]{2,1,0:T(8,128)}) custom-call(s32[1]{0:T(128)S(6)} %copy.15.lengths, s32[8]{0:T(128)} %bitcast.22, f32[128]{0:T(128)} %gains.1, bf16[128,4096]{1,0:T(8,128)(2,1)} %bitcast.16, ...), custom_call_target="tpu_custom_call" | custom-call | tf_op jit(solution)/shard_map/layer_pair/pallas_call | solution.py:493
  118.4 288.5 %place_outputs.1 = (bf16[128,4096]{1,0:T(8,128)(2,1)}, bf16[128,8192]{1,0:T(8,128)(2,1)}, bf16[8,16,64,256]{3,2,1,0:T(8,128)(2,1)}, bf16[8,4,2,16,1024]{4,3,2,1,0:T(8,128)(2,1)}, s32[4,8]{1,0:T(4,128)}) custom-call(bf16[128,4096]{1,0:T(8,128)(2,1)} %get-tuple-element.15.a, bf16[128,8192]{1,0:T(8,128)(2,1)} %get-tuple-element.16.b, ...), custom_call_target="tpu_custom_call" | custom-call | tf_op jit(solution)/shard_map/place_outputs/pallas_call | solution.py:571

commit v4 on v3

--- a/solution.py
+++ b/solution.py
@@ -148,10 +148,6 @@
                           col_peer(j)))
                 go(remote(v_ref.at[:, lanes], kv_in.at[my, mx, :, pl.ds(256, 256)], s_v.at[i], r_v.at[my],
                           col_peer(j)))
-            for i in ORDER:
-                j = mod4(my + i)
-                lanes = pl.ds(pl.multiple_of(j * 1024, 1024), 1024)
-                go(remote(q_ref.at[:, lanes], q_in.at[my], s_q.at[i], r_q.at[my], col_peer(j)))
             own = pl.ds(pl.multiple_of(my * 256, 256), 256)
             kv_in[my, mx, :, 0:256] = k_ref[:, own]
             kv_in[my, mx, :, 256:512] = v_ref[:, own]
@@ -248,7 +244,7 @@
             )
         t_out[u, at, :] = state.astype(BF16)
 
-    for u in range(2):
+    def take_inputs(u):
         for i in ORDER:
             j = mod4(mx + i)
             remote(
@@ -267,16 +263,31 @@
         t_in[u, my] = t_out[u, chunk_rows(my), :]
         if u == 0:
             w4_in[my] = wprod[3, pl.ds(pl.multiple_of(my * 8, 8), 8), :]
-            for i in ORDER:
-                j = mod4(my + i)
-                for z, (send, recv) in enumerate(((s_k, r_k), (s_v, r_v))):
-                    there = kv_in.at[j, mx, :, pl.ds(256 * z, 256)]
-                    remote(there, there, send.at[i], recv.at[j], col_peer(j)).wait_recv()
-            for i in (1, 3):
-                j = mod4(mx + i)
-                go(remote(kv_in.at[:, mx], kv_in.at[:, mx], s_kv.at[i], r_kv.at[mx], row_peer(j)))
-
-    for u in range(2):
+
+    def start_kv():
+        for i in ORDER:
+            j = mod4(my + i)
+            for z, (send, recv) in enumerate(((s_k, r_k), (s_v, r_v))):
+                there = kv_in.at[j, mx, :, pl.ds(256 * z, 256)]
+                remote(there, there, send.at[i], recv.at[j], col_peer(j)).wait_recv()
+        for i in (1, 3):
+            j = mod4(mx + i)
+            go(remote(kv_in.at[:, mx], kv_in.at[:, mx], s_kv.at[i], r_kv.at[mx], row_peer(j)))
+
+    def relay_kv():
+        for n, i in enumerate((1, 3)):
+            j = mod4(mx - i)
+            remote(kv_in.at[:, j], kv_in.at[:, j], s_kv.at[i], r_kv.at[j], row_peer(j)).wait_recv()
+            there = kv_in.at[pl.ds(2 * n, 2), j]
+            go(remote(there, there, s_kw.at[n], r_kw.at[n], row_peer(mod4(mx + i))))
+
+    def send_queries():
+        for i in ORDER:
+            j = mod4(my + i)
+            lanes = pl.ds(pl.multiple_of(j * 1024, 1024), 1024)
+            go(remote(q_ref.at[:, lanes], q_in.at[my], s_q.at[i], r_q.at[my], col_peer(j)))
+
+    def chain_rows(u):
         for i in ORDER:
             j = mod4(my + i)
             remote(t_in.at[u, j], t_in.at[u, j], s_t.at[u, i], r_t.at[u, j], col_peer(j)).wait_recv()
@@ -292,41 +303,88 @@
             go(remote(e0_out.at[u, j], e0_in.at[u, my], s_e0.at[u, i], r_e0.at[u, my], col_peer(j)))
         e0_in[u, my] = e0_out[u, my]
 
-    for n, i in enumerate((1, 3)):
-        j = mod4(mx - i)
-        remote(kv_in.at[:, j], kv_in.at[:, j], s_kv.at[i], r_kv.at[j], row_peer(j)).wait_recv()
-        there = kv_in.at[pl.ds(2 * n, 2), j]
-        go(remote(there, there, s_kw.at[n], r_kw.at[n], row_peer(mod4(mx + i))))
-
-    for u in range(2):
-        for d in (0, 1, 3, 2):
-            piece = mod4(my + d)
-            if d != 0:
-                remote(
-                    e0_in.at[u, piece], e0_in.at[u, piece], s_e0.at[u, d], r_e0.at[u, piece],
-                    col_peer(piece),
-                ).wait_recv()
-            at = chunk_rows(piece)
-            heads = pl.ds(piece * 8 + u * 4, 4)
-            e_out[u, 0, at, :] = e0_in[u, piece]
-            for k in range(1, 4):
-                e_out[u, k, at, :] = (
-                    e0_in[u, piece].astype(F32) * widen(wprod[k - 1, heads, :])
-                    + part[k - 1, u, at, :]
-                ).astype(BF16)
-            for i in ORDER:
-                j = mod4(mx + i)
-                go(remote(e_out.at[u, j, at, :], e_in.at[u, mx, at, :], s_e.at[u, d, i],
-                          r_e.at[u, mx, d], row_peer(j)))
-            e_in[u, mx, at, :] = e_out[u, mx, at, :]
-
-    for n in range(2):
-        there = kv_in.at[pl.ds(2 * n, 2), mod4(mx + 2)]
-        remote(there, there, s_kw.at[n], r_kw.at[n], row_peer(mod4(mx + 1))).wait_recv()
-    local_q.wait()
-    for i in ORDER:
-        j = mod4(my + i)
-        remote(q_in.at[j], q_in.at[j], s_q.at[i], r_q.at[j], col_peer(j)).wait_recv()
+    def enter(u, d):
+        piece = mod4(my + d)
+        if d != 0:
+            remote(
+                e0_in.at[u, piece], e0_in.at[u, piece], s_e0.at[u, d], r_e0.at[u, piece],
+                col_peer(piece),
+            ).wait_recv()
+        at = chunk_rows(piece)
+        heads = pl.ds(piece * 8 + u * 4, 4)
+        e_out[u, 0, at, :] = e0_in[u, piece]
+        for k in range(1, 4):
+            e_out[u, k, at, :] = (
+                e0_in[u, piece].astype(F32) * widen(wprod[k - 1, heads, :])
+                + part[k - 1, u, at, :]
+            ).astype(BF16)
+        for i in ORDER:
+            j = mod4(mx + i)
+            go(remote(e_out.at[u, j, at, :], e_in.at[u, mx, at, :], s_e.at[u, d, i],
+                      r_e.at[u, mx, d], row_peer(j)))
+        e_in[u, mx, at, :] = e_out[u, mx, at, :]
+
+    def snap_copies(u, d, j):
+        piece = mod4(my + d)
+        owner = 2 * j + piece // 2
+        half = lax.rem(piece, 2)
+        source = snap.at[j, pl.ds(piece * 8 + 4 * u, 4)]
+        target = pool_ref.at[rep, pl.ds(half * 8 + 4 * u, 4)]
+        return (
+            owner,
+            remote(source, target, s_p.at[u, d, j], r_p.at[rep, half, u], (ctx, owner)),
+            pltpu.make_async_copy(source, target, l_p.at[half, u]),
+        )
+
+    def finish(u, d, j):
+        piece = mod4(my + d)
+        at = chunk_rows(piece)
+        lanes = pl.ds(pl.multiple_of(j * NS, NS), NS)
+        entering = e_in[u, j, at, :]
+        mine = jnp.dot(ft[j, u, at, :], b_ref[:, lanes], preferred_element_type=F32)
+        factor = widen(wg[j, pl.ds(piece * 8 + u * 4, 4), :])
+        leaving = (mine + factor * entering.astype(F32)).astype(BF16)
+        snap[j, pl.ds(piece * 8 + u * 4, 4)] = leaving.reshape(4, MP, NS)
+        owner, away, here = snap_copies(u, d, j)
+        pl.when(owner != rep)(away.start)
+        pl.when(owner == rep)(here.start)
+        carried = lax.dot_general(
+            c_ref[:, lanes], entering, (((1,), (1,)), ((), ())), preferred_element_type=F32
+        )
+        for p in range(2):
+            scales = [
+                jnp.broadcast_to(
+                    ecum[j, piece * 2 + u, :, 2 * p + k : 2 * p + k + 1], (ROWS, 128)
+                )
+                for k in range(2)
+            ]
+            wide = pl.ds(pl.multiple_of(j * GW + piece * 512 + u * 256 + p * 128, 128), 128)
+            out_ref[:, wide] = (
+                inner[:, wide]
+                + jnp.where(low, scales[0], scales[1]) * carried[:, p * 128 : p * 128 + 128]
+            ).astype(BF16)
+
+    send_queries()
+    take_inputs(0)
+    start_kv()
+    chain_rows(0)
+    take_inputs(1)
+    steps = [(u, d) for u in range(2) for d in (0, 1, 3, 2)]
+    for step in steps[:3]:
+        enter(*step)
+        finish(*step, mx)
+    chain_rows(1)
+    relay_kv()
+
+
+    def wait_attention():
+        for n in range(2):
+            there = kv_in.at[pl.ds(2 * n, 2), mod4(mx + 2)]
+            remote(there, there, s_kw.at[n], r_kw.at[n], row_peer(mod4(mx + 1))).wait_recv()
+        local_q.wait()
+        for i in ORDER:
+            j = mod4(my + i)
+            remote(q_in.at[j], q_in.at[j], s_q.at[i], r_q.at[j], col_peer(j)).wait_recv()
 
     scale = math.log2(math.e) / math.sqrt(HD)
     key_off = lax.broadcasted_iota(jnp.int32, (1, 512), 1)
@@ -379,78 +437,35 @@
             pltpu.make_async_copy(a_out.at[i], target, l_a),
         )
 
-    def snap_copies(u, d, s):
-        piece = mod4(my + d)
-        j = mod4(mx + mz + s)
-        owner = 2 * j + piece // 2
-        half = lax.rem(piece, 2)
-        source = snap.at[j, pl.ds(piece * 8 + 4 * u, 4)]
-        target = pool_ref.at[rep, pl.ds(half * 8 + 4 * u, 4)]
-        return (
-            owner,
-            remote(source, target, s_p.at[u, d, s], r_p.at[rep, half, u], (ctx, owner)),
-            pltpu.make_async_copy(source, target, l_p.at[half, u]),
-        )
-
     units = [(3, 0), (3, 1), (2, 0), (2, 1), (1, 0), (1, 1), (0, 0), (0, 1)]
-    for u in range(2):
-        for d in (0, 1, 3, 2):
-            piece = mod4(my + d)
-            at = chunk_rows(piece)
-
-            def finish(s, carry):
-                j = mod4(mx + mz + s)
-
-                @pl.when(j != mx)
-                def _():
-                    remote(
-                        e_in.at[u, j, at, :], e_in.at[u, j, at, :], s_e.at[u, d, 1],
-                        r_e.at[u, j, d], row_peer(j),
-                    ).wait_recv()
-
-                lanes = pl.ds(pl.multiple_of(j * NS, NS), NS)
-                entering = e_in[u, j, at, :]
-                mine = jnp.dot(ft[j, u, at, :], b_ref[:, lanes], preferred_element_type=F32)
-                factor = widen(wg[j, pl.ds(piece * 8 + u * 4, 4), :])
-                leaving = (mine + factor * entering.astype(F32)).astype(BF16)
-                snap[j, pl.ds(piece * 8 + u * 4, 4)] = leaving.reshape(4, MP, NS)
-                owner, away, here = snap_copies(u, d, s)
-
-                @pl.when(owner != rep)
-                def _():
-                    away.start()
-
-                @pl.when(owner == rep)
-                def _():
-                    here.start()
-
-                carried = lax.dot_general(
-                    c_ref[:, lanes], entering, (((1,), (1,)), ((), ())),
-                    preferred_element_type=F32,
-                )
-                for p in range(2):
-                    scales = [
-                        jnp.broadcast_to(
-                            ecum[j, piece * 2 + u, :, 2 * p + k : 2 * p + k + 1], (ROWS, 128)
-                        )
-                        for k in range(2)
-                    ]
-                    wide = pl.ds(
-                        pl.multiple_of(j * GW + piece * 512 + u * 256 + p * 128, 128), 128
-                    )
-                    out_ref[:, wide] = (
-                        inner[:, wide]
-                        + jnp.where(low, scales[0], scales[1]) * carried[:, p * 128 : p * 128 + 128]
-                    ).astype(BF16)
-                return carry
-
-            lax.fori_loop(0, 4, finish, 0)
-            i, h = units.pop(0)
-            attend(i, h)
-            if h == 1:
-                away, here = a_copies(i)
-                pl.when(i != my)(away.start)
-                pl.when(i == my)(here.start)
+    for k, (u, d) in enumerate(steps):
+        at = chunk_rows(mod4(my + d))
+        for i in ORDER:
+            j = mod4(mx + i)
+            remote(
+                e_in.at[u, j, at, :], e_in.at[u, j, at, :], s_e.at[u, d, i], r_e.at[u, j, d],
+                row_peer(j),
+            ).wait_recv()
+        if k + 3 < 8:
+            enter(*steps[k + 3])
+
+        def finish_other(n, carry):
+            j = mod4(mx + mz + n)
+            pl.when(j != mx)(lambda: finish(u, d, j))
+            return carry
+
+        lax.fori_loop(0, 4, finish_other, 0)
+        if k + 3 < 8:
+            finish(*steps[k + 3], mx)
+        if k == 1:
+            wait_attention()
+        if k in (1, 2, 3, 4):
+            for i, h in (units.pop(0), units.pop(0)):
+                attend(i, h)
+                if h == 1:
+                    away, here = a_copies(i)
+                    pl.when(i != my)(away.start)
+                    pl.when(i == my)(here.start)
 
     for c in sent:
         c.wait_send()
@@ -461,8 +476,8 @@
     for u in range(2):
         for d in range(4):
 
-            def drain(s, carry):
-                owner, away, here = snap_copies(u, d, s)
+            def drain(j, carry):
+                owner, away, here = snap_copies(u, d, j)
                 pl.when(owner != rep)(away.wait_send)
                 pl.when(owner == rep)(here.wait)
                 return carry
@@ -549,19 +564,30 @@
     )(lengths, owners, gains, q, k, v, x, b, c, decay)
 
 
-def place_kernel(a, b, c, d, ids, a_out, b_out, c_out, d_out, ids_out, sems):
-    copies = []
-    for src, dst, parts in ((c, c_out, 8), (b, b_out, 4), (d, d_out, 4), (a, a_out, 2)):
+PARTS = (4, 4, 8, 8)
+
+
+def place_kernel(a, b, c, d, ids, a_out, b_out, c_out, d_out, ids_out, ta, tb, tc, td, s_in, s_out):
+    loads = []
+    stores = []
+    for src, mid, dst, parts in zip(
+        (a, b, c, d), (ta, tb, tc, td), (a_out, b_out, c_out, d_out), PARTS
+    ):
         size = src.shape[0] // parts
         for n in range(parts):
             at = pl.ds(n * size, size)
-            copies.append(pltpu.make_async_copy(src.at[at], dst.at[at], sems.at[len(copies)]))
-    for copy in copies:
-        copy.start()
+            k = len(loads)
+            loads.append(pltpu.make_async_copy(src.at[at], mid.at[at], s_in.at[k]))
+            stores.append(pltpu.make_async_copy(mid.at[at], dst.at[at], s_out.at[k]))
+    for load in loads:
+        load.start()
     turned = jnp.transpose(ids[:, 0, :].astype(F32))
     ids_out[...] = turned[:CAP].astype(jnp.int32)
-    for copy in copies:
-        copy.wait()
+    for load, store in zip(loads, stores):
+        load.wait()
+        store.start()
+    for store in stores:
+        store.wait()
 
 
 def place_call(*arrays):
@@ -573,7 +599,8 @@
         out_shape=(*shapes, jax.ShapeDtypeStruct((CAP, 8), jnp.int32)),
         in_specs=[far] * 4 + [vmem],
         out_specs=(far, far, far, far, vmem),
-        scratch_shapes=[pltpu.SemaphoreType.DMA((18,))],
+        scratch_shapes=[pltpu.VMEM(x.shape, x.dtype) for x in arrays[:4]]
+        + [pltpu.SemaphoreType.DMA((sum(PARTS),)), pltpu.SemaphoreType.DMA((sum(PARTS),))],
         compiler_params=pltpu.CompilerParams(vmem_limit_bytes=60 << 20),
         name="place_outputs",
     )(*arrays)

time: 408 us -> 123 us (0.30)
  Pallas kernels: 406 us -> 121 us
    pallas_call x1, Pallas kernels: 288 us -> 8.93 us  [place_call(): pl.pallas_call(place_kernel, out_shape=(*shapes, jax.ShapeDtypeStruct((CA...]
    pallas_call x1, Pallas kernels: 117 us -> 112 us  [pair_call(): pl.pallas_call(pair_kernel, out_shape=(jax.ShapeDtypeStruct((ROWS, 4096),...]
where the time goes in v4:
time: 123 us; the launch traced here: 122 us
  Pallas kernels  121 us (98%)
  between operations  1.45 us (1%)
    pallas_call x1, Pallas kernels, pair_call(): pl.pallas_call(pair_kernel, out_shape=(jax.ShapeDtypeStruct((ROWS, 4096),...  112 us
    pallas_call x1, Pallas kernels, place_call(): pl.pallas_call(place_kernel, out_shape=(*shapes, jax.ShapeDtypeStruct((CA...  8.93 us

profile of v4, /device:TPU:7, one launch (start us, length us, event | category | flops | bytes accessed | tf_op | source)
XLA Modules:
  0.0 122.1 jit_solution(916016063492347580)
XLA Ops:
  1.3 111.7 %layer_pair.1 = (bf16[128,4096]{1,0:T(8,128)(2,1)}, bf16[128,8192]{1,0:T(8,128)(2,1)}, bf16[8,16,64,256]{3,2,1,0:T(8,128)(2,1)}, bf16[8,4,2,16,1024]{4,3,2,1,0:T(8,128)(2,1)}, s32[8,8,128]{2,1,0:T(8,128)}) custom-call(s32[1]{0:T(128)S(6)} %copy.15.lengths, s32[8]{0:T(128)} %bitcast.22, f32[128]{0:T(128)} %gains.1, bf16[128,4096]{1,0:T(8,128)(2,1)} %bitcast.16, ...), custom_call_target="tpu_custom_call" | custom-call | tf_op jit(solution)/shard_map/layer_pair/pallas_call | solution.py:508
  113.0 8.9 %place_outputs.1 = (bf16[128,4096]{1,0:T(8,128)(2,1)}, bf16[128,8192]{1,0:T(8,128)(2,1)}, bf16[8,16,64,256]{3,2,1,0:T(8,128)(2,1)}, bf16[8,4,2,16,1024]{4,3,2,1,0:T(8,128)(2,1)}, s32[4,8]{1,0:T(4,128)}) custom-call(bf16[128,4096]{1,0:T(8,128)(2,1)} %get-tuple-element.15.a, bf16[128,8192]{1,0:T(8,128)(2,1)} %get-tuple-element.16.b, ...), custom_call_target="tpu_custom_call" | custom-call | tf_op jit(solution)/shard_map/place_outputs/pallas_call | solution.py:597

commit v5 on v4

--- a/solution.py
+++ b/solution.py
@@ -21,6 +21,7 @@
 F32 = jnp.float32
 BF16 = jnp.bfloat16
 ORDER = (1, 3, 2)
+UNITS = (0, 2, 2, 2, 2, 0, 0, 0)
 
 
 def mod4(v):
@@ -459,13 +460,13 @@
             finish(*steps[k + 3], mx)
         if k == 1:
             wait_attention()
-        if k in (1, 2, 3, 4):
-            for i, h in (units.pop(0), units.pop(0)):
-                attend(i, h)
-                if h == 1:
-                    away, here = a_copies(i)
-                    pl.when(i != my)(away.start)
-                    pl.when(i == my)(here.start)
+        for _ in range(UNITS[k]):
+            i, h = units.pop(0)
+            attend(i, h)
+            if h == 1:
+                away, here = a_copies(i)
+                pl.when(i != my)(away.start)
+                pl.when(i == my)(here.start)
 
     for c in sent:
         c.wait_send()
@@ -503,19 +504,19 @@
     def dma(*shape):
         return pltpu.SemaphoreType.DMA(shape)
 
+    far = pl.BlockSpec(memory_space=pl.ANY)
     vmem = pl.BlockSpec(memory_space=pltpu.VMEM)
-    far = pl.BlockSpec(memory_space=pl.ANY)
     return pl.pallas_call(
         pair_kernel,
         out_shape=(
-            jax.ShapeDtypeStruct((ROWS, 4096), BF16),
-            jax.ShapeDtypeStruct((ROWS, GR * GW), BF16),
-            jax.ShapeDtypeStruct((8, 16, MP, NS), BF16),
-            jax.ShapeDtypeStruct((8, CAP, 2, PAGE, 1024), BF16),
-            jax.ShapeDtypeStruct((8, 8, 128), jnp.int32),
+            pltpu.VMEM((ROWS, 4096), BF16),
+            pltpu.VMEM((ROWS, GR * GW), BF16),
+            pltpu.VMEM((8, 16, MP, NS), BF16),
+            pltpu.VMEM((8, CAP, 2, PAGE, 1024), BF16),
+            pltpu.VMEM((8, 8, 128), jnp.int32),
         ),
         in_specs=[pl.BlockSpec(memory_space=pltpu.SMEM)] * 3 + [far] * 7,
-        out_specs=(far, vmem, far, far, far),
+        out_specs=(vmem, vmem, vmem, vmem, vmem),
         scratch_shapes=[
             pltpu.VMEM((ROWS, 1024), BF16),
             pltpu.VMEM((ROWS, 1024), BF16),
@@ -558,34 +559,26 @@
             dma(2, 4, 4), dma(2, 4, 4), dma(2, 4, 4), dma(8, 2, 2),
         ],
         compiler_params=pltpu.CompilerParams(
-            collective_id=0, has_side_effects=True, vmem_limit_bytes=60 << 20
+            collective_id=0, has_side_effects=True, vmem_limit_bytes=50 << 20
         ),
         name="layer_pair",
     )(lengths, owners, gains, q, k, v, x, b, c, decay)
 
 
-PARTS = (4, 4, 8, 8)
-
-
-def place_kernel(a, b, c, d, ids, a_out, b_out, c_out, d_out, ids_out, ta, tb, tc, td, s_in, s_out):
-    loads = []
+PARTS = (2, 4, 8, 4)
+
+
+def place_kernel(a, b, c, d, ids, a_out, b_out, c_out, d_out, ids_out, sems):
     stores = []
-    for src, mid, dst, parts in zip(
-        (a, b, c, d), (ta, tb, tc, td), (a_out, b_out, c_out, d_out), PARTS
-    ):
+    for src, dst, parts in zip((c, b, d, a), (c_out, b_out, d_out, a_out), PARTS[::-1]):
         size = src.shape[0] // parts
         for n in range(parts):
             at = pl.ds(n * size, size)
-            k = len(loads)
-            loads.append(pltpu.make_async_copy(src.at[at], mid.at[at], s_in.at[k]))
-            stores.append(pltpu.make_async_copy(mid.at[at], dst.at[at], s_out.at[k]))
-    for load in loads:
-        load.start()
+            stores.append(pltpu.make_async_copy(src.at[at], dst.at[at], sems.at[len(stores)]))
+    for store in stores:
+        store.start()
     turned = jnp.transpose(ids[:, 0, :].astype(F32))
     ids_out[...] = turned[:CAP].astype(jnp.int32)
-    for load, store in zip(loads, stores):
-        load.wait()
-        store.start()
     for store in stores:
         store.wait()
 
@@ -597,11 +590,10 @@
     return pl.pallas_call(
         place_kernel,
         out_shape=(*shapes, jax.ShapeDtypeStruct((CAP, 8), jnp.int32)),
-        in_specs=[far] * 4 + [vmem],
+        in_specs=[vmem] * 5,
         out_specs=(far, far, far, far, vmem),
-        scratch_shapes=[pltpu.VMEM(x.shape, x.dtype) for x in arrays[:4]]
-        + [pltpu.SemaphoreType.DMA((sum(PARTS),)), pltpu.SemaphoreType.DMA((sum(PARTS),))],
-        compiler_params=pltpu.CompilerParams(vmem_limit_bytes=60 << 20),
+        scratch_shapes=[pltpu.SemaphoreType.DMA((sum(PARTS),))],
+        compiler_params=pltpu.CompilerParams(vmem_limit_bytes=40 << 20),
         name="place_outputs",
     )(*arrays)
 

time: 123 us -> 117 us (0.951)
  Pallas kernels: 121 us -> 115 us
    pallas_call x1, Pallas kernels: 8.93 us -> 4.33 us  [place_call(): pl.pallas_call(place_kernel, out_shape=(*shapes, jax.ShapeDtypeStruct((CA...]
    pallas_call x1, Pallas kernels: 112 us -> 110 us  [pair_call(): pl.pallas_call(pair_kernel, out_shape=(pltpu.VMEM((ROWS, 4096), BF16), pl...]
where the time goes in v5:
time: 117 us; the launch traced here: 116 us
  Pallas kernels  115 us (98%)
  between operations  1.45 us (1%)
    pallas_call x1, Pallas kernels, pair_call(): pl.pallas_call(pair_kernel, out_shape=(pltpu.VMEM((ROWS, 4096), BF16), pl...  110 us
    pallas_call x1, Pallas kernels, place_call(): pl.pallas_call(place_kernel, out_shape=(*shapes, jax.ShapeDtypeStruct((CA...  4.33 us

profile of v5, /device:TPU:7, one launch (start us, length us, event | category | flops | bytes accessed | tf_op | source)
XLA Modules:
  0.0 116.1 jit_solution(13457076089789969892)
XLA Ops:
  1.3 110.3 %layer_pair.1 = (bf16[128,4096]{1,0:T(8,128)(2,1)S(1)}, bf16[128,8192]{1,0:T(8,128)(2,1)S(1)}, bf16[8,16,64,256]{3,2,1,0:T(8,128)(2,1)S(1)}, bf16[8,4,2,16,1024]{4,3,2,1,0:T(8,128)(2,1)S(1)}, s32[8,8,128]{2,1,0:T(8,128)S(1)}) custom-call(s32[1]{0:T(128)S(6)} %copy.15.lengths, s32[8]{0:T(128)} %bitcast.22, f32[128]{0:T(128)} %gains.1, ...), custom_call_target="tpu_custom_call" | custom-call | tf_op jit(solution)/shard_map/layer_pair/pallas_call | solution.py:509
  111.6 4.3 %place_outputs.1 = (bf16[128,4096]{1,0:T(8,128)(2,1)}, bf16[128,8192]{1,0:T(8,128)(2,1)}, bf16[8,16,64,256]{3,2,1,0:T(8,128)(2,1)}, bf16[8,4,2,16,1024]{4,3,2,1,0:T(8,128)(2,1)}, s32[4,8]{1,0:T(4,128)}) custom-call(bf16[128,4096]{1,0:T(8,128)(2,1)S(1)} %get-tuple-element.15.a, bf16[128,8192]{1,0:T(8,128)(2,1)S(1)} %get-tuple-element.16.b, ...), custom_call_target="tpu_custom_call" | custom-call | tf_op jit(solution)/shard_map/place_outputs/pallas_call | solution.py:590

commit v6 on v5

--- a/solution.py
+++ b/solution.py
@@ -107,7 +107,6 @@
         for p in range(8):
             ecum[g, p] = grown[:, g * HG + p * 4 : g * HG + p * 4 + 4]
 
-    pl.semaphore_wait(barrier, 13)
     sent = []
 
     def go(copy):
@@ -130,6 +129,9 @@
 
     loads[1].wait()
     loads[2].wait()
+    for i in ORDER:
+        fade(mod4(mx + i), 0)
+    pl.semaphore_wait(barrier, 13)
     for u in range(2):
         for i in ORDER:
             j = mod4(mx + i)
@@ -137,7 +139,8 @@
                 lanes = pl.ds(pl.multiple_of(j * NS, NS), NS)
                 go(remote(b_ref.at[:, lanes], b_in.at[mx], s_b.at[i], r_b.at[mx], row_peer(j)))
                 go(remote(wg.at[j], w_in.at[mx], s_w.at[i], r_w.at[mx], row_peer(j)))
-            fade(j, u)
+            if u == 1:
+                fade(j, u)
             go(remote(ft.at[j, u], ft_in.at[mx, u], s_ft.at[u, i], r_ft.at[u, mx], row_peer(j)))
         if u == 0:
             loads[3].wait()
@@ -349,8 +352,12 @@
         owner, away, here = snap_copies(u, d, j)
         pl.when(owner != rep)(away.start)
         pl.when(owner == rep)(here.start)
+
+    def project(u, d, j):
+        piece = mod4(my + d)
+        lanes = pl.ds(pl.multiple_of(j * NS, NS), NS)
         carried = lax.dot_general(
-            c_ref[:, lanes], entering, (((1,), (1,)), ((), ())), preferred_element_type=F32
+            c_ref[:, lanes], e_in[u, j, chunk_rows(piece), :], (((1,), (1,)), ((), ())), preferred_element_type=F32
         )
         for p in range(2):
             scales = [
@@ -365,17 +372,17 @@
                 + jnp.where(low, scales[0], scales[1]) * carried[:, p * 128 : p * 128 + 128]
             ).astype(BF16)
 
-    send_queries()
     take_inputs(0)
     start_kv()
     chain_rows(0)
+    send_queries()
     take_inputs(1)
+    relay_kv()
     steps = [(u, d) for u in range(2) for d in (0, 1, 3, 2)]
     for step in steps[:3]:
         enter(*step)
         finish(*step, mx)
     chain_rows(1)
-    relay_kv()
 
 
     def wait_attention():
@@ -456,6 +463,12 @@
             return carry
 
         lax.fori_loop(0, 4, finish_other, 0)
+
+        def project_all(j, carry):
+            project(u, d, j)
+            return carry
+
+        lax.fori_loop(0, 4, project_all, 0)
         if k + 3 < 8:
             finish(*steps[k + 3], mx)
         if k == 1:

time: 117 us -> 116 us (level)
  no operation moved by 1% of the time
where the time goes in v6:
time: 116 us; the launch traced here: 115 us
  Pallas kernels  114 us (98%)
  between operations  1.45 us (1%)
    pallas_call x1, Pallas kernels, pair_call(): pl.pallas_call(pair_kernel, out_shape=(pltpu.VMEM((ROWS, 4096), BF16), pl...  110 us
    pallas_call x1, Pallas kernels, place_call(): pl.pallas_call(place_kernel, out_shape=(*shapes, jax.ShapeDtypeStruct((CA...  4.33 us

profile of v6, /device:TPU:7, one launch (start us, length us, event | category | flops | bytes accessed | tf_op | source)
XLA Modules:
  0.0 115.4 jit_solution(16278008604883904266)
XLA Ops:
  1.3 109.6 %layer_pair.1 = (bf16[128,4096]{1,0:T(8,128)(2,1)S(1)}, bf16[128,8192]{1,0:T(8,128)(2,1)S(1)}, bf16[8,16,64,256]{3,2,1,0:T(8,128)(2,1)S(1)}, bf16[8,4,2,16,1024]{4,3,2,1,0:T(8,128)(2,1)S(1)}, s32[8,8,128]{2,1,0:T(8,128)S(1)}) custom-call(s32[1]{0:T(128)S(6)} %copy.15.lengths, s32[8]{0:T(128)} %bitcast.22, f32[128]{0:T(128)} %gains.1, ...), custom_call_target="tpu_custom_call" | custom-call | tf_op jit(solution)/shard_map/layer_pair/pallas_call | solution.py:522
  110.9 4.3 %place_outputs.1 = (bf16[128,4096]{1,0:T(8,128)(2,1)}, bf16[128,8192]{1,0:T(8,128)(2,1)}, bf16[8,16,64,256]{3,2,1,0:T(8,128)(2,1)}, bf16[8,4,2,16,1024]{4,3,2,1,0:T(8,128)(2,1)}, s32[4,8]{1,0:T(4,128)}) custom-call(bf16[128,4096]{1,0:T(8,128)(2,1)S(1)} %get-tuple-element.15.a, bf16[128,8192]{1,0:T(8,128)(2,1)S(1)} %get-tuple-element.16.b, ...), custom_call_target="tpu_custom_call" | custom-call | tf_op jit(solution)/shard_map/place_outputs/pallas_call | solution.py:603

commit v7 on v6

--- a/solution.py
+++ b/solution.py
@@ -375,8 +375,8 @@
     take_inputs(0)
     start_kv()
     chain_rows(0)
+    take_inputs(1)
     send_queries()
-    take_inputs(1)
     relay_kv()
     steps = [(u, d) for u in range(2) for d in (0, 1, 3, 2)]
     for step in steps[:3]:

time: 116 us -> 116 us (level)
  no operation moved by 1% of the time
where the time goes in v7:
time: 116 us; the launch traced here: 115 us
  Pallas kernels  114 us (98%)
  between operations  1.45 us (1%)
    pallas_call x1, Pallas kernels, pair_call(): pl.pallas_call(pair_kernel, out_shape=(pltpu.VMEM((ROWS, 4096), BF16), pl...  110 us
    pallas_call x1, Pallas kernels, place_call(): pl.pallas_call(place_kernel, out_shape=(*shapes, jax.ShapeDtypeStruct((CA...  4.33 us

profile of v7, /device:TPU:7, one launch (start us, length us, event | category | flops | bytes accessed | tf_op | source)
XLA Modules:
  0.0 115.4 jit_solution(7879815967426636619)
XLA Ops:
  1.3 109.6 %layer_pair.1 = (bf16[128,4096]{1,0:T(8,128)(2,1)S(1)}, bf16[128,8192]{1,0:T(8,128)(2,1)S(1)}, bf16[8,16,64,256]{3,2,1,0:T(8,128)(2,1)S(1)}, bf16[8,4,2,16,1024]{4,3,2,1,0:T(8,128)(2,1)S(1)}, s32[8,8,128]{2,1,0:T(8,128)S(1)}) custom-call(s32[1]{0:T(128)S(6)} %copy.15.lengths, s32[8]{0:T(128)} %bitcast.22, f32[128]{0:T(128)} %gains.1, ...), custom_call_target="tpu_custom_call" | custom-call | tf_op jit(solution)/shard_map/layer_pair/pallas_call | solution.py:522
  110.9 4.3 %place_outputs.1 = (bf16[128,4096]{1,0:T(8,128)(2,1)}, bf16[128,8192]{1,0:T(8,128)(2,1)}, bf16[8,16,64,256]{3,2,1,0:T(8,128)(2,1)}, bf16[8,4,2,16,1024]{4,3,2,1,0:T(8,128)(2,1)}, s32[4,8]{1,0:T(4,128)}) custom-call(bf16[128,4096]{1,0:T(8,128)(2,1)S(1)} %get-tuple-element.15.a, bf16[128,8192]{1,0:T(8,128)(2,1)S(1)} %get-tuple-element.16.b, ...), custom_call_target="tpu_custom_call" | custom-call | tf_op jit(solution)/shard_map/place_outputs/pallas_call | solution.py:603
